TPU v7x, 128 devices: a whole 4x4x4 slice. The times are simulated.
128 devices in a mesh: struct: 32 (over x, y, core), basis: 4 (over z).
Axes of the slice: x: 4, y: 4, z: 4, core: 2. Of those that a mesh axis runs over, the one named last changes fastest.
Arguments:
- dist: float32 [32, 4096], P(None, 'struct'), may hold values from 0.8 to 4.8
- nbr_species: int32 [32, 4096], P(None, 'struct'), may hold values from 0 to 8
- species: int32 [4096], P('struct'), may hold values from 0 to 7
- counts: int32 [256], P('struct'), may hold values from 4 to 16
- pattern: int32 [8, 8], replicated, may hold values 0 or 1
- projections: bfloat16 [4, 64, 100352], P(None, None, 'basis'), may hold values from -0.75 to 0.75
- energies: float32 [256], P('struct'), may hold values from -6 to 6
Outputs:
- coefficients: float32 [100352], P('basis')
- row_direction: float32 [256], P('struct')
Inputs may be any that keep to these rules, and one draw needn't show every extreme that they name: `nbr_species`: the value 8 marks an empty neighbour slot.
All inputs are finite; a program needn't handle non-finite values.
Results may differ from a plain program's by a relative error of at most 0.0003.
The roundings to bfloat16 on the way count: a program that leaves them out, or rounds other values in their place, can miss the bound.
Values may be sent and summed in bfloat16 or wider, within the bound.
No kernel may reach another device: no remote copies, remote signals or barrier semaphores. Data moves between devices by JAX's collectives and lax.ppermute only.
A program may use at most 128 MiB of HBM per device.

v0:
```python
import jax
import jax.numpy as jnp
from jax import lax
from jax.sharding import PartitionSpec as P

SPECIES = 8
RADIAL = 8
FACTORS = 4
K_SPEC = 12544
MAXAT = 16
ITERS = 4
K = 100352


HIGH = lax.Precision.HIGHEST
CUTOFF = 5.0


def atomic_basis(dist, nbr_species, species, pattern):
    kinds = jnp.arange(SPECIES, dtype=jnp.int32)
    ratio = dist / CUTOFF
    envelope = (1.0 - ratio) * (1.0 - ratio)
    orders = jnp.arange(RADIAL, dtype=jnp.int32).astype(jnp.float32)
    radial = envelope[None] * jnp.cos(jnp.pi * orders[:, None, None] * ratio[None])
    center = (species[None, :] == kinds[:, None]).astype(jnp.float32)
    allowed = jnp.dot(pattern.astype(jnp.float32).T, center, precision=HIGH)
    match = (nbr_species[None] == kinds[:, None, None]).astype(jnp.float32) * allowed[:, None, :]
    atomic = jnp.einsum("ena,rna->aer", match, radial, precision=HIGH)
    return atomic.reshape(atomic.shape[0], SPECIES * RADIAL).astype(jnp.bfloat16)


def atom_weight(counts):
    slots = jnp.arange(counts.shape[0] * MAXAT, dtype=jnp.int32) % MAXAT
    per_atom = jnp.repeat(counts, MAXAT)
    weight = jnp.where(slots < per_atom, 1.0 / per_atom.astype(jnp.float32), jnp.float32(0.0))
    return weight


def build_rows(atomic, weight, species, columns, elements):
    product = jnp.dot(atomic, columns[0], preferred_element_type=jnp.float32)
    for factor in range(1, FACTORS):
        product = product * jnp.dot(atomic, columns[factor], preferred_element_type=jnp.float32)
    scale = jnp.where(species[:, None] == elements[None, :], weight[:, None], jnp.float32(0.0))
    terms = product * scale
    return terms.reshape(-1, MAXAT, columns.shape[2]).sum(axis=1)


def body(dist, nbr_species, species, counts, pattern, projections, energies):
    atomic = atomic_basis(dist, nbr_species, species, pattern)
    k_local = projections.shape[2]
    base_column = lax.axis_index("basis") * k_local
    weight = atom_weight(counts)
    elements = (base_column + jnp.arange(k_local, dtype=jnp.int32)) // K_SPEC

    def evaluate():
        return build_rows(atomic, weight, species, projections, elements)

    def row_square(left):
        return lax.psum(jnp.sum(left * left), "struct")

    def coef_square(vector):
        return lax.psum(jnp.sum(vector * vector), "basis")

    def adjoint(design, left):
        return lax.psum(jnp.dot(left, design, precision=HIGH), "struct")

    def current():
        return evaluate()

    design = current()
    beta = jnp.sqrt(row_square(energies))
    left = energies / beta
    right = adjoint(design, left)
    alpha = jnp.sqrt(coef_square(right))
    right = right / alpha
    search = right
    iterate = jnp.zeros_like(right)
    phibar = beta
    rhobar = alpha
    for step_index in range(ITERS):
        design = current()
        left = lax.psum(jnp.dot(design, right, precision=HIGH), "basis") - alpha * left
        beta = jnp.sqrt(row_square(left))
        left = left / beta
        right = adjoint(design, left) - beta * right
        alpha = jnp.sqrt(coef_square(right))
        right = right / alpha
        rho = jnp.sqrt(rhobar * rhobar + beta * beta)
        cosine = rhobar / rho
        sine = beta / rho
        theta = sine * alpha
        rhobar = -cosine * alpha
        advance = cosine * phibar
        phibar = sine * phibar
        iterate = iterate + advance / rho * search
        search = right - theta / rho * search
    total = coef_square(iterate)
    scaled = iterate * (jnp.sqrt(jnp.float32(K)) / jnp.sqrt(total))
    row_count = energies.shape[0] * lax.axis_size("struct")
    row_direction = left * jnp.sqrt(jnp.float32(row_count))
    return (scaled, row_direction)


def solution(mesh):
    placed = (
        P(None, "struct"),
        P(None, "struct"),
        P("struct"),
        P("struct"),
        P(),
        P(None, None, "basis"),
        P("struct"),
    )
    return jax.shard_map(
        body, mesh=mesh, in_specs=placed, out_specs=(P("basis"), P("struct")), check_vma=False
    )
```

profile of v0, /device:TPU:1, one launch (start us, length us, event | category | flops | bytes accessed | tf_op | source)
XLA Modules:
  0.0 873.5 jit_solution(4466369010516044104)
XLA Ops:
  9.9 3.0 convolution_convert_fusion
  13.1 8.4 fusion.4
  21.5 7.5 convolution_multiply_fusion.2
  29.0 8.5 convolution_multiply_fusion.1
  38.3 64.6 %psum.126 = f32[]{:T(128)} all-reduce(f32[]{:T(128)} %multiply_reduce_fusion.9), channel_id=1, replica_groups=mesh['struct'=32,'basis'=4] {'struct'}, use_global_device_ids=true, to_apply=%region_1.2 | all-reduce | flops 1 | bytes 8 | tf_op jit(solution)/shard_map/psum | solution.py:59
  103.6 10.0 %bitcast_reduce_fusion = f32[8,25088]{1,0:T(8,128)S(1)} fusion(f32[128]{0:T(128)S(1)} %compare_select_fusion, s32[25088]{0:T(1024)S(1)} %add_select_fusion, s32[128]{0:T(128)S(1)} %copy-done.1, f32[128,25088]{1,0:T(8,128)} %convolution_multiply_fusion.1, bf16[4,64,25088]{2,1,0:T(8,128)(2,1)} %param.12, bf16[128,8,8]{0,2,1:T(8,128)(2,1)S(1)} %copy.15), kind=kOutput, calls=%fused_computation.4 | convolution fusion | flops 426897408 | bytes 16976896 | tf_op jit(solution)/shard_map/dot_general | solution.py:42
  115.3 100.4 %all-reduce.5.cloned.1.call-done = f32[25088]{0:T(1024)} async-done(((f32[25088]{0:T(1024)}), f32[25088]{0:T(1024)}) %all-reduce.5.cloned.1.call-update) | async-done | bytes 100368 | tf_op jit(solution)/shard_map/psum | solution.py:65
  217.2 9.3 %psum.128 = f32[]{:T(128)} all-reduce(f32[]{:T(128)} %multiply_reduce_fusion.4), channel_id=1, replica_groups=mesh['struct'=32,'basis'=4] {'basis'}, use_global_device_ids=true, to_apply=%region_5.6 | all-reduce | flops 1 | bytes 8 | tf_op jit(solution)/shard_map/psum | solution.py:62
  228.2 1.8 convolution_bitcast_fusion.4
  230.0 6.0 psum.129
  236.6 66.4 %psum.130 = f32[]{:T(128)} all-reduce(f32[]{:T(128)} %multiply_reduce_fusion.8), channel_id=1, replica_groups=mesh['struct'=32,'basis'=4] {'struct'}, use_global_device_ids=true, to_apply=%region_8.9 | all-reduce | flops 1 | bytes 8 | tf_op jit(solution)/shard_map/psum | solution.py:59
  305.3 94.0 %all-reduce.7.cloned.1.call-done = f32[25088]{0:T(1024)} async-done(((f32[25088]{0:T(1024)}), f32[25088]{0:T(1024)}) %all-reduce.7.cloned.1.call-update) | async-done | bytes 100368 | tf_op jit(solution)/shard_map/psum | solution.py:65
  400.9 9.3 %psum.132 = f32[]{:T(128)} all-reduce(f32[]{:T(128)} %multiply_reduce_fusion.3), channel_id=1, replica_groups=mesh['struct'=32,'basis'=4] {'basis'}, use_global_device_ids=true, to_apply=%region_11.12 | all-reduce | flops 1 | bytes 8 | tf_op jit(solution)/shard_map/psum | solution.py:62
  413.8 6.0 psum.133
  420.4 66.4 %psum.134 = f32[]{:T(128)} all-reduce(f32[]{:T(128)} %multiply_reduce_fusion.7), channel_id=1, replica_groups=mesh['struct'=32,'basis'=4] {'struct'}, use_global_device_ids=true, to_apply=%region_14.15 | all-reduce | flops 1 | bytes 8 | tf_op jit(solution)/shard_map/psum | solution.py:59
  489.1 94.0 %all-reduce.9.cloned.1.call-done = f32[25088]{0:T(1024)} async-done(((f32[25088]{0:T(1024)}), f32[25088]{0:T(1024)}) %all-reduce.9.cloned.1.call-update) | async-done | bytes 100368 | tf_op jit(solution)/shard_map/psum | solution.py:65
  584.6 9.3 %psum.136 = f32[]{:T(128)} all-reduce(f32[]{:T(128)} %multiply_reduce_fusion.2), channel_id=1, replica_groups=mesh['struct'=32,'basis'=4] {'basis'}, use_global_device_ids=true, to_apply=%region_17.18 | all-reduce | flops 1 | bytes 8 | tf_op jit(solution)/shard_map/psum | solution.py:62
  597.4 6.0 psum.137
  604.0 66.6 %psum.138 = f32[]{:T(128)} all-reduce(f32[]{:T(128)} %multiply_reduce_fusion.6), channel_id=1, replica_groups=mesh['struct'=32,'basis'=4] {'struct'}, use_global_device_ids=true, to_apply=%region_20.21 | all-reduce | flops 1 | bytes 8 | tf_op jit(solution)/shard_map/psum | solution.py:59
  673.4 93.5 %all-reduce.11.cloned.1.call-done = f32[25088]{0:T(1024)} async-done(((f32[25088]{0:T(1024)}), f32[25088]{0:T(1024)}) %all-reduce.11.cloned.1.call-update) | async-done | bytes 100368 | tf_op jit(solution)/shard_map/psum | solution.py:65
  768.5 9.3 %psum.140 = f32[]{:T(128)} all-reduce(f32[]{:T(128)} %multiply_reduce_fusion.1), channel_id=1, replica_groups=mesh['struct'=32,'basis'=4] {'basis'}, use_global_device_ids=true, to_apply=%region_23.24 | all-reduce | flops 1 | bytes 8 | tf_op jit(solution)/shard_map/psum | solution.py:62
  781.4 6.0 psum.141
  788.0 66.4 %psum.142 = f32[]{:T(128)} all-reduce(f32[]{:T(128)} %multiply_reduce_fusion.5), channel_id=1, replica_groups=mesh['struct'=32,'basis'=4] {'struct'}, use_global_device_ids=true, to_apply=%region_26.27 | all-reduce | flops 1 | bytes 8 | tf_op jit(solution)/shard_map/psum | solution.py:59
  857.3 8.3 psum.143
  (55 shorter events, 31.2 us)
Async XLA Ops:
  7.2 208.5 %all-reduce.5.cloned.1.call-start = ((), (), s32[]{:S(2)}) async-start(), calls=%async_computation | async-start | bytes 204800 | tf_op jit(solution)/shard_map/psum | solution.py:65
  29.0 8.6 copy-start.2
  29.0 8.7 copy-start
  29.0 74.6 %copy-start.1 = (s32[128]{0:T(128)S(1)}, s32[128]{0:T(128)}, u32[]{:S(2)}) copy-start(s32[128]{0:T(128)} %param.9) | copy-start | bytes 1540
  115.3 284.1 %all-reduce.7.cloned.1.call-start = ((), (), s32[]{:S(2)}) async-start(), calls=%async_computation.1 | async-start | bytes 204800 | tf_op jit(solution)/shard_map/psum | solution.py:65
  305.3 277.8 %all-reduce.9.cloned.1.call-start = ((), (), s32[]{:S(2)}) async-start(), calls=%async_computation.2 | async-start | bytes 204800 | tf_op jit(solution)/shard_map/psum | solution.py:65
  489.0 277.9 %all-reduce.11.cloned.1.call-start = ((), (), s32[]{:S(2)}) async-start(), calls=%async_computation.3 | async-start | bytes 204800 | tf_op jit(solution)/shard_map/psum | solution.py:65
Sparse Core Ops, SparseCore 0:
  115.4 100.2 all-reduce.4
  305.4 93.8 all-reduce.6
  489.2 93.8 all-reduce.8
  673.0 93.8 all-reduce.10
where the time goes:
time: 876 us; the launch traced here: 874 us
  blocking collectives  400 us (46%)
  waiting for transfers between devices  382 us (44%)
  matrix products  52 us (6%)
  between operations  21.7 us (2%)
  other arithmetic  16.5 us (2%)
    psum x4, waiting for transfers between devices, adjoint(): return lax.psum(jnp.dot(left, design, precision=HIGH), 'struct')  382 us
    psum x5, blocking collectives, row_square(): return lax.psum(jnp.sum(left * left), 'struct')  330 us
    psum x5, blocking collectives, coef_square(): return lax.psum(jnp.sum(vector * vector), 'basis')  45.4 us
    dot_general x3, matrix products, build_rows(): jnp.dot(atomic, columns[factor], preferred_element_type=jnp.float32)  25.9 us
    psum x4, blocking collectives, body(): lax.psum(jnp.dot(design, right, precision=HIGH), 'basis') - alpha * left  24 us
  transfers between devices with their start and end apart: 4, of which 4 were waited for; matrix products, arithmetic and copies ran while one was open for 0% of the time, Pallas kernels for 0%

commit v1 on v0

v1 whole, which is shorter than its diff:
```python
import functools
import math

import jax
import jax.numpy as jnp
from jax import lax
from jax.experimental import pallas as pl
from jax.experimental.pallas import tpu as pltpu
from jax.sharding import Mesh, PartitionSpec as P

SPECIES = 8
RADIAL = 8
FACTORS = 4
CHANNELS = 64
K_SPEC = 12544
MAXAT = 16
ITERS = 4
K = 100352
STRUCTS = 256

LANES = 128
WIDTH = 896
PER_SPEC = K_SPEC // WIDTH
LOCAL = 8
BLOCK = LOCAL * MAXAT
PACKED = 72
CODE, COUNT, ENERGY = 64, 65, 66
GROUP = 32

STRUCT = ("chip", "core")
CUTOFF = 5.0
PI_HIGH = 3.140625
PI_MID = 0.0009670257568359375
PI_LOW = math.pi - PI_HIGH - PI_MID
COS_TERMS = tuple((-1.0) ** n / math.factorial(2 * n) for n in range(9))


def cosine(angle):
    turns = jnp.floor(angle * (1.0 / math.pi) + 0.5)
    rest = angle - turns * PI_HIGH
    rest = rest - turns * PI_MID
    rest = rest - turns * PI_LOW
    square = rest * rest
    value = jnp.full_like(square, COS_TERMS[-1])
    for term in COS_TERMS[-2::-1]:
        value = value * square + term
    odd = turns - 2.0 * jnp.floor(turns * 0.5)
    return value * (1.0 - 2.0 * odd)


def atomic_kernel(dist_ref, nbr_ref, species_ref, counts_ref, pattern_ref, energies_ref, out_ref):
    ratio = dist_ref[...] / CUTOFF
    envelope = (1.0 - ratio) * (1.0 - ratio)
    nbr = nbr_ref[...]
    species = species_ref[...]
    radial = []
    for order in range(RADIAL):
        if order == 0:
            radial.append(envelope)
        else:
            radial.append(envelope * cosine((jnp.float32(math.pi) * jnp.float32(order)) * ratio))
    rows = []
    for element in range(SPECIES):
        allowed = jnp.zeros(species.shape, jnp.float32)
        for center in range(SPECIES):
            seen = pattern_ref[center, element].astype(jnp.float32)
            allowed = jnp.where(species == center, seen, allowed)
        match = jnp.where(nbr == element, allowed, 0.0)
        for order in range(RADIAL):
            rows.append(jnp.sum(match * radial[order], axis=0, keepdims=True))
    atomic = jnp.concatenate(rows, axis=0).astype(jnp.bfloat16)

    lane = lax.broadcasted_iota(jnp.int32, (1, LANES), 1)
    slots = lane % MAXAT
    per_atom = jnp.zeros((1, LANES), jnp.int32)
    count = jnp.zeros((1, LANES), jnp.float32)
    energy = jnp.zeros((1, LANES), jnp.float32)
    for structure in range(LOCAL):
        amount = counts_ref[structure]
        per_atom = jnp.where(lane // MAXAT == structure, amount, per_atom)
        count = jnp.where(lane == structure, amount.astype(jnp.float32), count)
        energy = jnp.where(lane == structure, energies_ref[structure], energy)
    code = jnp.where(slots < per_atom, species, SPECIES).astype(jnp.float32)
    parts = [code, count]
    for _ in range(3):
        part = energy.astype(jnp.bfloat16).astype(jnp.float32)
        parts.append(part)
        energy = energy - part
    parts.append(jnp.zeros((PACKED - CHANNELS - len(parts), LANES), jnp.float32))
    packed = jnp.concatenate([atomic, jnp.concatenate(parts, axis=0).astype(jnp.bfloat16)], axis=0)
    for copy in range(out_ref.shape[0]):
        out_ref[copy, :, :] = packed


def atomic_call(dist, nbr_species, species, counts, pattern, energies, copies):
    vmem = pl.BlockSpec(memory_space=pltpu.VMEM)
    smem = pl.BlockSpec(memory_space=pltpu.SMEM)
    return pl.pallas_call(
        atomic_kernel,
        out_shape=jax.ShapeDtypeStruct((copies, PACKED, LANES), jnp.bfloat16),
        in_specs=[vmem, vmem, vmem, smem, smem, smem],
        out_specs=vmem,
        name="atomic",
    )(dist, nbr_species, species.reshape(1, -1), counts, pattern, energies)


def maps_kernel(maps_ref, out_ref):
    for left in range(0, WIDTH, LANES):
        for factor in range(FACTORS):
            turned = maps_ref[factor, :, left : left + LANES].astype(jnp.float32).T.astype(jnp.bfloat16)
            for half in range(LANES // GROUP):
                row = ((left // GROUP + half) * FACTORS + factor) * GROUP
                out_ref[row : row + GROUP, :] = turned[half * GROUP : (half + 1) * GROUP]


def maps_call(maps):
    vmem = pl.BlockSpec(memory_space=pltpu.VMEM)
    return pl.pallas_call(
        maps_kernel,
        out_shape=jax.ShapeDtypeStruct((FACTORS * WIDTH, CHANNELS), jnp.bfloat16),
        in_specs=[vmem],
        out_specs=vmem,
        compiler_params=pltpu.CompilerParams(vmem_limit_bytes=8 * 1024 * 1024),
        cost_estimate=pl.CostEstimate(flops=0, bytes_accessed=1400000, transcendentals=0),
        name="maps",
    )(maps)


def upto_each(element, atoms_ref):
    codes = atoms_ref[:, CODE, :].astype(jnp.float32)
    lane = lax.broadcasted_iota(jnp.int32, codes.shape, 1)
    chosen = jnp.where(codes == element, 1.0, 0.0)
    upto = chosen
    for reach in (1, 2, 4, 8):
        upto = upto + jnp.where(lane % MAXAT >= reach, pltpu.roll(upto, reach, 1), 0.0)
    return chosen, upto


def move_atoms(chosen, upto, atoms_ref, ranked_ref):
    structure = lax.broadcasted_iota(jnp.int32, chosen.shape, 1) // MAXAT
    target = jnp.where(chosen > 0.0, (upto - 1.0) * LOCAL + structure.astype(jnp.float32), -1.0).astype(jnp.bfloat16)
    rows = lax.broadcasted_iota(jnp.int32, (BLOCK, LANES), 0).astype(jnp.float32).astype(jnp.bfloat16)
    one, zero = jnp.ones(rows.shape, jnp.bfloat16), jnp.zeros(rows.shape, jnp.bfloat16)
    for chip in range(atoms_ref.shape[0]):
        move = jnp.where(jnp.broadcast_to(target[chip : chip + 1, :], rows.shape) == rows, one, zero)
        moved = lax.dot_general(
            move, atoms_ref[chip, :CHANNELS, :], (((1,), (1,)), ((), ())), preferred_element_type=jnp.float32
        )
        for rank in range(MAXAT):
            ranked_ref[rank, chip * LOCAL : (chip + 1) * LOCAL, :] = moved[rank * LOCAL : (rank + 1) * LOCAL]


def ranked_kernel(where_ref, own_ref, ranked_ref):
    move_atoms(*upto_each(where_ref[0].astype(jnp.float32), own_ref), own_ref, ranked_ref)


def ranked_call(where, own):
    vmem = pl.BlockSpec(memory_space=pltpu.VMEM)
    return pl.pallas_call(
        ranked_kernel,
        out_shape=jax.ShapeDtypeStruct((MAXAT, own.shape[0] * LOCAL, CHANNELS), jnp.float32),
        in_specs=[pl.BlockSpec(memory_space=pltpu.SMEM), vmem],
        out_specs=vmem,
        compiler_params=pltpu.CompilerParams(vmem_limit_bytes=8 * 1024 * 1024),
        cost_estimate=pl.CostEstimate(flops=40000000, bytes_accessed=1400000, transcendentals=0),
        name="ranked",
    )(where, own)


def design_kernel(where_ref, own_ref, other_ref, first_ref, maps_ref, high_ref, low_ref, gram_ref, second_ref, design_ref):
    element = where_ref[0].astype(jnp.float32)
    core = where_ref[2]
    chosen, upto = upto_each(element, other_ref)
    ranks = jnp.max(jnp.maximum(upto, upto_each(element, own_ref)[1])).astype(jnp.int32)
    move_atoms(chosen, upto, other_ref, second_ref)
    over = (((1,), (1,)), ((), ()))
    design_ref[...] = jnp.zeros(design_ref.shape, jnp.float32)

    def terms(atoms, left):
        columns = maps_ref[left * FACTORS : (left + GROUP) * FACTORS, :]
        values = lax.dot_general(columns, atoms, over, preferred_element_type=jnp.float32)
        product = values[:GROUP]
        for factor in range(1, FACTORS):
            product = product * values[factor * GROUP : (factor + 1) * GROUP]
        return product

    def add_ranks(first, amount):
        atoms = []
        for rank in range(amount):
            own, other = first_ref[first + rank], second_ref[first + rank]
            halves = [jnp.where(core == 0, own, other), jnp.where(core == 0, other, own)]
            atoms.append(jnp.concatenate(halves, axis=0).astype(jnp.bfloat16))
        for left in range(0, WIDTH, GROUP):
            design_ref[left : left + GROUP, :] += sum(terms(operand, left) for operand in atoms)

    def add_fours(turn, carry):
        add_ranks(turn * 4, 4)
        return carry

    lax.fori_loop(0, ranks // 4, add_fours, 0)

    @pl.when(ranks % 4 >= 2)
    def _():
        add_ranks(ranks // 4 * 4, 2)

    @pl.when(ranks % 2 == 1)
    def _():
        add_ranks(ranks - 1, 1)

    design = design_ref[...]
    high = design.astype(jnp.bfloat16)
    low = (design - high.astype(jnp.float32)).astype(jnp.bfloat16)
    high_ref[...] = high
    low_ref[...] = low
    down = (((0,), (0,)), ((), ()))
    gram = lax.dot_general(high, high, down, preferred_element_type=jnp.float32)
    gram += lax.dot_general(high, low, down, preferred_element_type=jnp.float32)
    gram += lax.dot_general(low, high, down, preferred_element_type=jnp.float32)
    for left in range(0, STRUCTS, LANES):
        gram_ref[left // LANES * STRUCTS : (left // LANES + 1) * STRUCTS, :] = gram[:, left : left + LANES]


def design_call(where, own, other, ranked, maps):
    vmem = pl.BlockSpec(memory_space=pltpu.VMEM)
    return pl.pallas_call(
        design_kernel,
        out_shape=(
            jax.ShapeDtypeStruct((WIDTH, STRUCTS), jnp.bfloat16),
            jax.ShapeDtypeStruct((WIDTH, STRUCTS), jnp.bfloat16),
            jax.ShapeDtypeStruct((STRUCTS * STRUCTS // LANES, LANES), jnp.float32),
        ),
        in_specs=[pl.BlockSpec(memory_space=pltpu.SMEM)] + [vmem] * 4,
        out_specs=(vmem, vmem, vmem),
        scratch_shapes=[
            pltpu.VMEM((MAXAT, STRUCTS // 2, CHANNELS), jnp.float32),
            pltpu.VMEM((WIDTH, STRUCTS), jnp.float32),
        ],
        compiler_params=pltpu.CompilerParams(vmem_limit_bytes=24 * 1024 * 1024),
        name="design",
    )(where, own, other, ranked, maps)


def total_kernel(parts_ref, out_ref):
    parts = parts_ref[...]
    out_ref[...] = jnp.broadcast_to(jnp.sum(parts, axis=0, keepdims=True), parts.shape)


def total_call(parts):
    vmem = pl.BlockSpec(memory_space=pltpu.VMEM)
    return pl.pallas_call(
        total_kernel,
        out_shape=jax.ShapeDtypeStruct(parts.shape, parts.dtype),
        in_specs=[vmem],
        out_specs=vmem,
        compiler_params=pltpu.CompilerParams(vmem_limit_bytes=4 * 1024 * 1024),
        name="total",
    )(parts)


def split(value, amount):
    parts = []
    for _ in range(amount):
        part = value.astype(jnp.bfloat16)
        parts.append(part)
        value = value - part.astype(jnp.float32)
    return parts


def stacked(vector):
    first, second, third = [part.astype(jnp.float32) for part in split(vector, 3)]
    row = lax.broadcasted_iota(jnp.int32, (16, vector.shape[1]), 0)
    one = jnp.where(row == 0, first, 0.0)
    two = jnp.where(row == 1, second, one)
    three = jnp.where(row == 2, third, two)
    return [operand.astype(jnp.bfloat16) for operand in (three, two)]


def picked(own_ref, other_ref, core):
    chips = own_ref.shape[0]
    kinds = (COUNT, ENERGY, ENERGY + 1, ENERGY + 2)
    parts = [half[:, kind, :].astype(jnp.float32) for kind in kinds for half in (own_ref, other_ref)]
    parts = jnp.concatenate(parts, axis=0).astype(jnp.bfloat16)
    structure = lax.broadcasted_iota(jnp.int32, (LANES, STRUCTS), 1)
    repeat = structure % LOCAL == lax.broadcasted_iota(jnp.int32, (LANES, STRUCTS), 0)
    parts = jnp.dot(parts, jnp.where(repeat, 1.0, 0.0).astype(jnp.bfloat16), preferred_element_type=jnp.float32)
    block = lax.broadcasted_iota(jnp.int32, (2 * chips, STRUCTS), 0)
    block = block % chips + jnp.where(block < chips, core, 1 - core) * chips
    here = block == lax.broadcasted_iota(jnp.int32, (2 * chips, STRUCTS), 1) // LOCAL
    rows = [
        jnp.sum(jnp.where(here, parts[kind * 2 * chips : (kind + 1) * 2 * chips], 0.0), axis=0, keepdims=True)
        for kind in range(len(kinds))
    ]
    return rows[0], rows[1] + rows[2] + rows[3]


def solve_kernel(where_ref, gram_ref, own_ref, other_ref, high_ref, low_ref, coefficients_ref, direction_ref):
    counts, energies = picked(own_ref, other_ref, where_ref[2])
    inverse = 1.0 / counts
    gram = split(jnp.concatenate([gram_ref[:STRUCTS, :], gram_ref[STRUCTS:, :]], axis=1), 2)

    def dot(a, b):
        return jnp.sum(a * b, axis=1, keepdims=True)

    def apply(vector):
        image = jnp.zeros((16, STRUCTS), jnp.float32)
        for operand, part in zip(stacked(vector * inverse), gram):
            image = image + jnp.dot(operand, part, preferred_element_type=jnp.float32)
        return jnp.sum(image, axis=0, keepdims=True) * inverse

    image = apply(energies)
    square = dot(energies, energies)
    shrink = lax.rsqrt(square)
    beta = square * shrink
    left = energies * shrink
    right = left
    image = image * shrink
    square = dot(right, image)
    shrink = lax.rsqrt(square)
    alpha = square * shrink
    right, image = right * shrink, image * shrink
    search, search_image = right, image
    iterate = jnp.zeros_like(right)
    iterate_image = iterate
    phibar = beta
    rhobar = alpha
    for step in range(ITERS):
        left = image - alpha * left
        left_image = apply(left) if step < ITERS - 1 else None
        square = dot(left, left)
        shrink = lax.rsqrt(square)
        beta = square * shrink
        left = left * shrink
        over_rho = lax.rsqrt(rhobar * rhobar + square)
        cosine_part = rhobar * over_rho
        sine_part = beta * over_rho
        advance = cosine_part * phibar * over_rho
        phibar = sine_part * phibar
        iterate = iterate + advance * search
        iterate_image = iterate_image + advance * search_image
        if step < ITERS - 1:
            right = left - beta * right
            image = left_image * shrink - beta * image
            square = dot(right, image)
            shrink = lax.rsqrt(square)
            alpha = square * shrink
            right, image = right * shrink, image * shrink
            turn = sine_part * alpha * over_rho
            rhobar = -cosine_part * alpha
            search = right - turn * search
            search_image = image - turn * search_image
    iterate = iterate * (math.sqrt(K) * lax.rsqrt(dot(iterate, iterate_image))) * inverse
    over = (((1,), (1,)), ((), ()))
    values = jnp.zeros((16, WIDTH), jnp.float32)
    for operand, part in zip(stacked(iterate), (high_ref[...], low_ref[...])):
        values = values + lax.dot_general(operand, part, over, preferred_element_type=jnp.float32)
    values = jnp.sum(values, axis=0, keepdims=True)
    rows = jnp.concatenate([values[:, at : at + LANES] for at in range(0, WIDTH, LANES)], axis=0)
    for copy in range(coefficients_ref.shape[0]):
        coefficients_ref[copy] = rows
    direction = jnp.broadcast_to(left * math.sqrt(STRUCTS), (8, STRUCTS))
    direction_ref[...] = pltpu.roll(direction, STRUCTS - where_ref[1] * LOCAL, 1)[:1, :LOCAL]


def solve_call(where, gram, own, other, high, low, copies):
    vmem = pl.BlockSpec(memory_space=pltpu.VMEM)
    return pl.pallas_call(
        solve_kernel,
        out_shape=(
            jax.ShapeDtypeStruct((copies, WIDTH // LANES, LANES), jnp.float32),
            jax.ShapeDtypeStruct((1, LOCAL), jnp.float32),
        ),
        in_specs=[pl.BlockSpec(memory_space=pltpu.SMEM)] + [vmem] * 5,
        out_specs=(vmem, vmem),
        compiler_params=pltpu.CompilerParams(vmem_limit_bytes=16 * 1024 * 1024),
        name="solve",
    )(where, gram, own, other, high, low)


def swap(value):
    return lax.ppermute(value, "core", [(0, 1), (1, 0)])


def body(dist, nbr_species, species, counts, pattern, projections, energies):
    struct = lax.axis_index(STRUCT)
    basis = lax.axis_index("basis")
    structs = lax.axis_size(STRUCT)
    k_local = projections.shape[2]
    owners = k_local // WIDTH
    mine = jnp.minimum(struct, owners - 1)
    element = jnp.where(struct < owners, (basis * owners + struct) // PER_SPEC, SPECIES + 1)
    core, chips = lax.axis_index("core"), lax.axis_size("chip")
    where = jnp.stack([element, core * chips + lax.axis_index("chip"), core]).astype(jnp.int32)

    packed = atomic_call(dist, nbr_species, species, counts, pattern, energies, chips)
    own = lax.all_to_all(packed, "chip", 0, 0)
    maps = maps_call(lax.dynamic_slice_in_dim(projections, mine * WIDTH, WIDTH, 2))
    own, maps, where = lax.optimization_barrier((own, maps, where))
    other = swap(own)
    ranked = ranked_call(where, own)
    high, low, gram = design_call(where, own, other, ranked, maps)
    everyone = ("chip", "core", "basis")
    parts = lax.all_to_all(gram.reshape(lax.axis_size(everyone), -1, LANES), everyone, 0, 0)
    gram = lax.all_to_all(total_call(parts), everyone, 0, 0).reshape(-1, LANES)
    values, direction = solve_call(where, gram, own, other, high, low, structs)
    values = lax.all_to_all(values, STRUCT, 0, 0)
    return (values[:owners].reshape(-1), direction.reshape(-1))


def solution(mesh):
    chips = Mesh(mesh.devices.reshape(-1, 2, mesh.shape["basis"]), ("chip", "core", "basis"))
    placed = (
        P(None, STRUCT),
        P(None, STRUCT),
        P(STRUCT),
        P(STRUCT),
        P(),
        P(None, None, "basis"),
        P(STRUCT),
    )
    return jax.shard_map(
        body, mesh=chips, in_specs=placed, out_specs=(P("basis"), P(STRUCT)), check_vma=False
    )
```

time: 876 us -> 75.3 us (0.09)
  waiting for transfers between devices: 382 us -> 6.15 us
  blocking collectives: 400 us -> 46 us
  matrix products: 52 us -> 0 us
  between operations: 21.7 us -> 0.73 us
  other arithmetic: 16.5 us -> 0.08 us
  Pallas kernels: 0 us -> 10.5 us
  starting transfers between devices: 0.16 us -> 9.81 us
    psum x14 -> x0, blocking collectives: 400 us -> none  [the longest x5 330 us: row_square(): return lax.psum(jnp.sum(left * left), 'struct')]
    psum x4 -> x0, waiting for transfers between devices: 382 us -> none  [adjoint(): return lax.psum(jnp.dot(left, design, precision=HIGH), 'struct')]
    dot_general x14 -> x0, matrix products: 52 us -> none  [the longest x3 25.9 us: build_rows(): jnp.dot(atomic, columns[factor], preferred_element_type=jnp.float32)]
    all_to_all x0 -> x3, blocking collectives: none -> 46 us  [the longest x1 19.2 us: body(): lax.all_to_all(gram.reshape(lax.axis_size(everyone), -1, LANES), everyone...]
    reduce_sum x10 -> x0, other arithmetic: 10.8 us -> none  [the longest x5 7.73 us: coef_square(): return lax.psum(jnp.sum(vector * vector), 'basis')]
    pallas_call x0 -> x6, Pallas kernels: none -> 10.5 us  [the longest x1 4.56 us: design_call(): pl.pallas_call(design_kernel, out_shape=(jax.ShapeDtypeStruct((WIDTH, STR...]
  transfers between devices with their start and end apart: 4 -> 2, of which waited for: 4 -> 2; matrix products, arithmetic and copies ran while one was open for 0% -> 2% of each run, Pallas kernels for 0% -> 2%
where the time goes in v1:
time: 75.3 us; the launch traced here: 75 us
  blocking collectives  46 us (61%)
  Pallas kernels  10.5 us (14%)
  starting transfers between devices  9.81 us (13%)
  waiting for transfers between devices  6.15 us (8%)
  local copies, waits for them, and re-layouts  1.72 us (2%)
    all_to_all x1, blocking collectives, body(): lax.all_to_all(gram.reshape(lax.axis_size(everyone), -1, LANES), everyone...  19.2 us
    all_to_all x1, blocking collectives, body(): gram = lax.all_to_all(total_call(parts), everyone, 0, 0).reshape(-1, LANES)  15.2 us
    all_to_all x1, blocking collectives, body(): values = lax.all_to_all(values, STRUCT, 0, 0)  11.6 us
    all_to_all x1, starting transfers between devices, body(): own = lax.all_to_all(packed, 'chip', 0, 0)  7.58 us
    all_to_all x1, waiting for transfers between devices, body(): own = lax.all_to_all(packed, 'chip', 0, 0)  6.05 us
    pallas_call x1, Pallas kernels, design_call(): pl.pallas_call(design_kernel, out_shape=(jax.ShapeDtypeStruct((WIDTH, STR...  4.56 us
    pallas_call x1, Pallas kernels, solve_call(): pl.pallas_call(solve_kernel, out_shape=(jax.ShapeDtypeStruct((copies, WID...  2.52 us
    ppermute x1, starting transfers between devices, swap(): return lax.ppermute(value, 'core', [(0, 1), (1, 0)])  2.23 us
  transfers between devices with their start and end apart: 2, of which 2 were waited for; matrix products, arithmetic and copies ran while one was open for 2% of the time, Pallas kernels for 2%

profile of v1, /device:TPU:1, one launch (start us, length us, event | category | flops | bytes accessed | tf_op | source)
XLA Modules:
  0.0 75.0 jit_solution(15936496762081241869)
XLA Ops:
  0.6 1.9 %atomic.1 = bf16[16,72,128]{2,1,0:T(8,128)(2,1)} custom-call(f32[32,128]{1,0:T(8,128)} %dist_ref.1, s32[32,128]{1,0:T(8,128)} %nbr_ref.1, s32[1,128]{1,0:T(1,128)} %bitcast.9, s32[8]{0:T(128)} %counts_ref.1, s32[8,8]{1,0:T(8,128)} %pattern_ref.1, f32[8]{0:T(128)} %energies_ref.1), custom_call_target="tpu_custom_call" | custom-call | tf_op jit(solution)/shard_map/atomic/pallas_call | solution.py:98
  2.5 7.6 %all-to-all-start = ((bf16[16,72,128]{2,1,0:T(8,128)(2,1)}), bf16[16,72,128]{2,1,0:T(8,128)(2,1)S(1)}, u32[]{:S(2)}, u32[]{:S(2)}) async-start(bf16[16,72,128]{2,1,0:T(8,128)(2,1)} %atomic.1), calls=%async_computation | async-start | bytes 589824 | tf_op jit(solution)/shard_map/all_to_all | solution.py:395
  10.1 1.1 %constant_dynamic-slice_fusion.maps_ref = bf16[4,64,896]{2,1,0:T(8,128)(2,1)S(1)} fusion(bf16[4,64,25088]{2,1,0:T(8,128)(2,1)} %param.12, s32[]{:T(128)S(6)} %select_n.12), kind=kLoop, calls=%fused_computation.1 | loop fusion | bytes 917508 | tf_op jit(solution)/shard_map/dynamic_slice | solution.py:396
  11.2 0.3 maps.1.maps_ref
  11.6 0.1 pad_add_fusion.where_ref
  11.6 6.0 %all-to-all-done.own_ref = bf16[16,72,128]{2,1,0:T(8,128)(2,1)S(1)} async-done(((bf16[16,72,128]{2,1,0:T(8,128)(2,1)}), bf16[16,72,128]{2,1,0:T(8,128)(2,1)S(1)}, u32[]{:S(2)}, u32[]{:S(2)}) %all-to-all-start) | async-done | bytes 294944 | tf_op jit(solution)/shard_map/all_to_all | solution.py:395
  17.7 2.2 %collective-permute-start = (bf16[16,72,128]{2,1,0:T(8,128)(2,1)S(1)}, bf16[16,72,128]{2,1,0:T(8,128)(2,1)S(1)}, u32[]{:S(2)}, u32[]{:S(2)}) collective-permute-start(bf16[16,72,128]{2,1,0:T(8,128)(2,1)S(1)} %all-to-all-done.own_ref), channel_id=1, source_target_pairs={{0,4},{4,0},{1,5},{5,1},{2,6},{6,2},{3,7},{7,3},{8,12},{12,8},{9,1... | collective-permute-start | bytes 884744 | tf_op jit(solution)/shard_map/ppermute | solution.py:380
  19.9 1.1 %ranked.1.first_ref = f32[16,128,64]{2,1,0:T(8,128)S(1)} custom-call(s32[3]{0:T(128)S(1)} %pad_add_fusion.where_ref, bf16[16,72,128]{2,1,0:T(8,128)(2,1)S(1)} %all-to-all-done.own_ref), custom_call_target="tpu_custom_call" | custom-call | flops 40000000 | bytes 1400000 | tf_op jit(solution)/shard_map/ranked/pallas_call | solution.py:159
  21.0 0.1 collective-permute-done.other_ref
  21.1 4.6 %design.1 = (bf16[896,256]{1,0:T(8,128)(2,1)S(1)}, bf16[896,256]{1,0:T(8,128)(2,1)S(1)}, f32[512,128]{1,0:T(8,128)S(1)}) custom-call(s32[3]{0:T(128)S(1)} %pad_add_fusion.where_ref, bf16[16,72,128]{2,1,0:T(8,128)(2,1)S(1)} %all-to-all-done.own_ref, bf16[16,72,128]{2,1,0:T(8,128)(2,1)S(1)} %collective-permute-done.other_ref, ...), custom_call_target="tpu_custom_call" | custom-call | tf_op jit(solution)/shard_map/design/pallas_call | solution.py:225
  25.7 19.2 %all_to_all.20.parts_ref = f32[128,4,128]{2,1,0:T(4,128)S(1)} all-to-all(f32[128,4,128]{2,1,0:T(4,128)S(1)} %bitcast.8), channel_id=1, replica_groups=mesh['chip'=16,'core'=2,'basis'=4] {'chip','core','basis'}, dimensions={0} | all-to-all | bytes 524288 | tf_op jit(solution)/shard_map/all_to_all | solution.py:402
  44.9 0.2 total.1
  45.1 15.2 %all_to_all.21 = f32[128,4,128]{2,1,0:T(4,128)S(1)} all-to-all(f32[128,4,128]{2,1,0:T(4,128)S(1)} %total.1), channel_id=1, replica_groups=mesh['chip'=16,'core'=2,'basis'=4] {'chip','core','basis'}, dimensions={0} | all-to-all | bytes 524288 | tf_op jit(solution)/shard_map/all_to_all | solution.py:403
  60.3 2.5 %solve.1 = (f32[32,7,128]{2,1,0:T(8,128)S(1)}, f32[1,8]{1,0:T(1,128)}) custom-call(s32[3]{0:T(128)S(1)} %pad_add_fusion.where_ref, f32[512,128]{1,0:T(8,128)S(1)} %bitcast.7, bf16[16,72,128]{2,1,0:T(8,128)(2,1)S(1)} %all-to-all-done.own_ref, bf16[16,72,128]{2,1,0:T(8,128)(2,1)S(1)} %collective-permute-done.other_ref, ...), custom_call_target="tpu_custom_call" | custom-call | tf_op jit(solution)/shard_map/solve/pallas_call | solution.py:366
  62.8 11.6 %all_to_all.22 = f32[32,7,128]{2,1,0:T(8,128)S(1)} all-to-all(f32[32,7,128]{2,1,0:T(8,128)S(1)} %get-tuple-element.16), channel_id=1, replica_groups=mesh['chip'=16,'core'=2,'basis'=4] {'chip','core'}, dimensions={0} | all-to-all | bytes 229376 | tf_op jit(solution)/shard_map/all_to_all | solution.py:405
  74.3 0.7 reshape.22
  (1 shorter events, 0.0 us)
Async XLA Ops:
  2.5 15.2 %all-to-all-start = ((bf16[16,72,128]{2,1,0:T(8,128)(2,1)}), bf16[16,72,128]{2,1,0:T(8,128)(2,1)S(1)}, u32[]{:S(2)}, u32[]{:S(2)}) async-start(bf16[16,72,128]{2,1,0:T(8,128)(2,1)} %atomic.1), calls=%async_computation | async-start | bytes 589824 | tf_op jit(solution)/shard_map/all_to_all | solution.py:395
  17.7 3.4 %collective-permute-start = (bf16[16,72,128]{2,1,0:T(8,128)(2,1)S(1)}, bf16[16,72,128]{2,1,0:T(8,128)(2,1)S(1)}, u32[]{:S(2)}, u32[]{:S(2)}) collective-permute-start(bf16[16,72,128]{2,1,0:T(8,128)(2,1)S(1)} %all-to-all-done.own_ref), channel_id=1, source_target_pairs={{0,4},{4,0},{1,5},{5,1},{2,6},{6,2},{3,7},{7,3},{8,12},{12,8},{9,1... | collective-permute-start | bytes 884744 | tf_op jit(solution)/shard_map/ppermute | solution.py:380

commit v2 on v1

--- a/solution.py
+++ b/solution.py
@@ -126,6 +126,14 @@
     )(maps)
 
 
+def place():
+    core, chips = lax.axis_index("core"), lax.axis_size("chip")
+    struct = lax.axis_index("chip") * 2 + core
+    owners = SPECIES // lax.axis_size("basis") * PER_SPEC
+    element = lax.div(lax.axis_index("basis") * owners + struct, PER_SPEC)
+    return core, core * chips + lax.axis_index("chip"), jnp.where(struct < owners, element, SPECIES + 1)
+
+
 def upto_each(element, atoms_ref):
     codes = atoms_ref[:, CODE, :].astype(jnp.float32)
     lane = lax.broadcasted_iota(jnp.int32, codes.shape, 1)
@@ -150,26 +158,26 @@
             ranked_ref[rank, chip * LOCAL : (chip + 1) * LOCAL, :] = moved[rank * LOCAL : (rank + 1) * LOCAL]
 
 
-def ranked_kernel(where_ref, own_ref, ranked_ref):
-    move_atoms(*upto_each(where_ref[0].astype(jnp.float32), own_ref), own_ref, ranked_ref)
-
-
-def ranked_call(where, own):
+def ranked_kernel(own_ref, ranked_ref):
+    move_atoms(*upto_each(place()[2].astype(jnp.float32), own_ref), own_ref, ranked_ref)
+
+
+def ranked_call(own):
     vmem = pl.BlockSpec(memory_space=pltpu.VMEM)
     return pl.pallas_call(
         ranked_kernel,
         out_shape=jax.ShapeDtypeStruct((MAXAT, own.shape[0] * LOCAL, CHANNELS), jnp.float32),
-        in_specs=[pl.BlockSpec(memory_space=pltpu.SMEM), vmem],
+        in_specs=[vmem],
         out_specs=vmem,
         compiler_params=pltpu.CompilerParams(vmem_limit_bytes=8 * 1024 * 1024),
         cost_estimate=pl.CostEstimate(flops=40000000, bytes_accessed=1400000, transcendentals=0),
         name="ranked",
-    )(where, own)
-
-
-def design_kernel(where_ref, own_ref, other_ref, first_ref, maps_ref, high_ref, low_ref, gram_ref, second_ref, design_ref):
-    element = where_ref[0].astype(jnp.float32)
-    core = where_ref[2]
+    )(own)
+
+
+def design_kernel(own_ref, other_ref, first_ref, maps_ref, high_ref, low_ref, gram_ref, second_ref, design_ref):
+    core, _, element = place()
+    element = element.astype(jnp.float32)
     chosen, upto = upto_each(element, other_ref)
     ranks = jnp.max(jnp.maximum(upto, upto_each(element, own_ref)[1])).astype(jnp.int32)
     move_atoms(chosen, upto, other_ref, second_ref)
@@ -220,7 +228,7 @@
         gram_ref[left // LANES * STRUCTS : (left // LANES + 1) * STRUCTS, :] = gram[:, left : left + LANES]
 
 
-def design_call(where, own, other, ranked, maps):
+def design_call(own, other, ranked, maps):
     vmem = pl.BlockSpec(memory_space=pltpu.VMEM)
     return pl.pallas_call(
         design_kernel,
@@ -229,7 +237,7 @@
             jax.ShapeDtypeStruct((WIDTH, STRUCTS), jnp.bfloat16),
             jax.ShapeDtypeStruct((STRUCTS * STRUCTS // LANES, LANES), jnp.float32),
         ),
-        in_specs=[pl.BlockSpec(memory_space=pltpu.SMEM)] + [vmem] * 4,
+        in_specs=[vmem] * 4,
         out_specs=(vmem, vmem, vmem),
         scratch_shapes=[
             pltpu.VMEM((MAXAT, STRUCTS // 2, CHANNELS), jnp.float32),
@@ -237,7 +245,7 @@
         ],
         compiler_params=pltpu.CompilerParams(vmem_limit_bytes=24 * 1024 * 1024),
         name="design",
-    )(where, own, other, ranked, maps)
+    )(own, other, ranked, maps)
 
 
 def total_kernel(parts_ref, out_ref):
@@ -293,8 +301,9 @@
     return rows[0], rows[1] + rows[2] + rows[3]
 
 
-def solve_kernel(where_ref, gram_ref, own_ref, other_ref, high_ref, low_ref, coefficients_ref, direction_ref):
-    counts, energies = picked(own_ref, other_ref, where_ref[2])
+def solve_kernel(gram_ref, own_ref, other_ref, high_ref, low_ref, coefficients_ref, direction_ref):
+    core, number, _ = place()
+    counts, energies = picked(own_ref, other_ref, core)
     inverse = 1.0 / counts
     gram = split(jnp.concatenate([gram_ref[:STRUCTS, :], gram_ref[STRUCTS:, :]], axis=1), 2)
 
@@ -358,10 +367,10 @@
     for copy in range(coefficients_ref.shape[0]):
         coefficients_ref[copy] = rows
     direction = jnp.broadcast_to(left * math.sqrt(STRUCTS), (8, STRUCTS))
-    direction_ref[...] = pltpu.roll(direction, STRUCTS - where_ref[1] * LOCAL, 1)[:1, :LOCAL]
-
-
-def solve_call(where, gram, own, other, high, low, copies):
+    direction_ref[...] = pltpu.roll(direction, STRUCTS - number * LOCAL, 1)[:1, :LOCAL]
+
+
+def solve_call(gram, own, other, high, low, copies):
     vmem = pl.BlockSpec(memory_space=pltpu.VMEM)
     return pl.pallas_call(
         solve_kernel,
@@ -369,11 +378,11 @@
             jax.ShapeDtypeStruct((copies, WIDTH // LANES, LANES), jnp.float32),
             jax.ShapeDtypeStruct((1, LOCAL), jnp.float32),
         ),
-        in_specs=[pl.BlockSpec(memory_space=pltpu.SMEM)] + [vmem] * 5,
+        in_specs=[vmem] * 5,
         out_specs=(vmem, vmem),
         compiler_params=pltpu.CompilerParams(vmem_limit_bytes=16 * 1024 * 1024),
         name="solve",
-    )(where, gram, own, other, high, low)
+    )(gram, own, other, high, low)
 
 
 def swap(value):
@@ -382,26 +391,21 @@
 
 def body(dist, nbr_species, species, counts, pattern, projections, energies):
     struct = lax.axis_index(STRUCT)
-    basis = lax.axis_index("basis")
     structs = lax.axis_size(STRUCT)
-    k_local = projections.shape[2]
-    owners = k_local // WIDTH
+    owners = projections.shape[2] // WIDTH
     mine = jnp.minimum(struct, owners - 1)
-    element = jnp.where(struct < owners, (basis * owners + struct) // PER_SPEC, SPECIES + 1)
-    core, chips = lax.axis_index("core"), lax.axis_size("chip")
-    where = jnp.stack([element, core * chips + lax.axis_index("chip"), core]).astype(jnp.int32)
-
-    packed = atomic_call(dist, nbr_species, species, counts, pattern, energies, chips)
+
+    packed = atomic_call(dist, nbr_species, species, counts, pattern, energies, lax.axis_size("chip"))
     own = lax.all_to_all(packed, "chip", 0, 0)
     maps = maps_call(lax.dynamic_slice_in_dim(projections, mine * WIDTH, WIDTH, 2))
-    own, maps, where = lax.optimization_barrier((own, maps, where))
+    own, maps = lax.optimization_barrier((own, maps))
     other = swap(own)
-    ranked = ranked_call(where, own)
-    high, low, gram = design_call(where, own, other, ranked, maps)
+    ranked = ranked_call(own)
+    high, low, gram = design_call(own, other, ranked, maps)
     everyone = ("chip", "core", "basis")
     parts = lax.all_to_all(gram.reshape(lax.axis_size(everyone), -1, LANES), everyone, 0, 0)
     gram = lax.all_to_all(total_call(parts), everyone, 0, 0).reshape(-1, LANES)
-    values, direction = solve_call(where, gram, own, other, high, low, structs)
+    values, direction = solve_call(gram, own, other, high, low, structs)
     values = lax.all_to_all(values, STRUCT, 0, 0)
     return (values[:owners].reshape(-1), direction.reshape(-1))
 

time: 75.3 us -> 73.6 us (0.977)
  blocking collectives: 46 us -> 41.9 us
  Pallas kernels: 10.5 us -> 12.2 us
    all_to_all x1, blocking collectives: 19.2 us -> 15.2 us  [body(): lax.all_to_all(gram.reshape(lax.axis_size(everyone), -1, LANES), everyone...]
    pallas_call x1, Pallas kernels: 4.56 us -> 7.27 us  [design_call(): pl.pallas_call(design_kernel, out_shape=(jax.ShapeDtypeStruct((WIDTH, STR...]
  transfers between devices with their start and end apart: 2 -> 2, of which waited for: 2 -> 2; matrix products, arithmetic and copies ran while one was open for 2% -> 1% of each run, Pallas kernels for 2% -> 1%
where the time goes in v2:
time: 73.6 us; the launch traced here: 73.2 us
  blocking collectives  41.9 us (57%)
  Pallas kernels  12.2 us (17%)
  starting transfers between devices  9.81 us (13%)
  waiting for transfers between devices  6.81 us (9%)
  local copies, waits for them, and re-layouts  1.72 us (2%)
    all_to_all x1, blocking collectives, body(): lax.all_to_all(gram.reshape(lax.axis_size(everyone), -1, LANES), everyone...  15.2 us
    all_to_all x1, blocking collectives, body(): gram = lax.all_to_all(total_call(parts), everyone, 0, 0).reshape(-1, LANES)  15.2 us
    all_to_all x1, blocking collectives, body(): values = lax.all_to_all(values, STRUCT, 0, 0)  11.6 us
    all_to_all x1, starting transfers between devices, body(): own = lax.all_to_all(packed, 'chip', 0, 0)  7.58 us
    pallas_call x1, Pallas kernels, design_call(): pl.pallas_call(design_kernel, out_shape=(jax.ShapeDtypeStruct((WIDTH, STR...  7.27 us
    all_to_all x1, waiting for transfers between devices, body(): own = lax.all_to_all(packed, 'chip', 0, 0)  6.17 us
    ppermute x1, starting transfers between devices, swap(): return lax.ppermute(value, 'core', [(0, 1), (1, 0)])  2.23 us
    pallas_call x1, Pallas kernels, solve_call(): pl.pallas_call(solve_kernel, out_shape=(jax.ShapeDtypeStruct((copies, WID...  1.98 us
  transfers between devices with their start and end apart: 2, of which 2 were waited for; matrix products, arithmetic and copies ran while one was open for 1% of the time, Pallas kernels for 1%

profile of v2, /device:TPU:1, one launch (start us, length us, event | category | flops | bytes accessed | tf_op | source)
XLA Modules:
  0.0 73.2 jit_solution(7717219135817549840)
XLA Ops:
  0.6 1.9 %atomic.1 = bf16[16,72,128]{2,1,0:T(8,128)(2,1)} custom-call(f32[32,128]{1,0:T(8,128)} %dist_ref.1, s32[32,128]{1,0:T(8,128)} %nbr_ref.1, s32[1,128]{1,0:T(1,128)} %bitcast.6, s32[8]{0:T(128)} %counts_ref.1, s32[8,8]{1,0:T(8,128)} %pattern_ref.1, f32[8]{0:T(128)} %energies_ref.1), custom_call_target="tpu_custom_call" | custom-call | tf_op jit(solution)/shard_map/atomic/pallas_call | solution.py:98
  2.5 7.6 %all-to-all-start = ((bf16[16,72,128]{2,1,0:T(8,128)(2,1)}), bf16[16,72,128]{2,1,0:T(8,128)(2,1)S(1)}, u32[]{:S(2)}, u32[]{:S(2)}) async-start(bf16[16,72,128]{2,1,0:T(8,128)(2,1)} %atomic.1), calls=%async_computation | async-start | bytes 589824 | tf_op jit(solution)/shard_map/all_to_all | solution.py:399
  10.1 1.1 %constant_dynamic-slice_fusion.maps_ref = bf16[4,64,896]{2,1,0:T(8,128)(2,1)S(1)} fusion(bf16[4,64,25088]{2,1,0:T(8,128)(2,1)} %param.12, s32[]{:T(128)S(6)} %select_n.3), kind=kLoop, calls=%fused_computation | loop fusion | bytes 917508 | tf_op jit(solution)/shard_map/dynamic_slice | solution.py:400
  11.2 0.3 maps.1.maps_ref
  11.5 6.2 %all-to-all-done.own_ref = bf16[16,72,128]{2,1,0:T(8,128)(2,1)S(1)} async-done(((bf16[16,72,128]{2,1,0:T(8,128)(2,1)}), bf16[16,72,128]{2,1,0:T(8,128)(2,1)S(1)}, u32[]{:S(2)}, u32[]{:S(2)}) %all-to-all-start) | async-done | bytes 294944 | tf_op jit(solution)/shard_map/all_to_all | solution.py:399
  17.7 2.2 %collective-permute-start = (bf16[16,72,128]{2,1,0:T(8,128)(2,1)S(1)}, bf16[16,72,128]{2,1,0:T(8,128)(2,1)S(1)}, u32[]{:S(2)}, u32[]{:S(2)}) collective-permute-start(bf16[16,72,128]{2,1,0:T(8,128)(2,1)S(1)} %all-to-all-done.own_ref), channel_id=1, source_target_pairs={{0,4},{4,0},{1,5},{5,1},{2,6},{6,2},{3,7},{7,3},{8,12},{12,8},{9,1... | collective-permute-start | bytes 884744 | tf_op jit(solution)/shard_map/ppermute | solution.py:389
  19.9 0.6 ranked.1.first_ref
  20.5 0.6 collective-permute-done.other_ref
  21.1 7.3 %design.1 = (bf16[896,256]{1,0:T(8,128)(2,1)S(1)}, bf16[896,256]{1,0:T(8,128)(2,1)S(1)}, f32[512,128]{1,0:T(8,128)S(1)}) custom-call(bf16[16,72,128]{2,1,0:T(8,128)(2,1)S(1)} %all-to-all-done.own_ref, bf16[16,72,128]{2,1,0:T(8,128)(2,1)S(1)} %collective-permute-done.other_ref, f32[16,128,64]{2,1,0:T(8,128)S(1)} %ranked.1.first_ref, ...), custom_call_target="tpu_custom_call" | custom-call | tf_op jit(solution)/shard_map/design/pallas_call | solution.py:233
  28.4 15.2 %all_to_all.20.parts_ref = f32[128,4,128]{2,1,0:T(4,128)S(1)} all-to-all(f32[128,4,128]{2,1,0:T(4,128)S(1)} %bitcast.5), channel_id=1, replica_groups=mesh['chip'=16,'core'=2,'basis'=4] {'chip','core','basis'}, dimensions={0} | all-to-all | bytes 524288 | tf_op jit(solution)/shard_map/all_to_all | solution.py:406
  43.6 0.2 total.1
  43.8 15.2 %all_to_all.21 = f32[128,4,128]{2,1,0:T(4,128)S(1)} all-to-all(f32[128,4,128]{2,1,0:T(4,128)S(1)} %total.1), channel_id=1, replica_groups=mesh['chip'=16,'core'=2,'basis'=4] {'chip','core','basis'}, dimensions={0} | all-to-all | bytes 524288 | tf_op jit(solution)/shard_map/all_to_all | solution.py:407
  59.0 2.0 %solve.1 = (f32[32,7,128]{2,1,0:T(8,128)S(1)}, f32[1,8]{1,0:T(1,128)}) custom-call(f32[512,128]{1,0:T(8,128)S(1)} %bitcast.4, bf16[16,72,128]{2,1,0:T(8,128)(2,1)S(1)} %all-to-all-done.own_ref, bf16[16,72,128]{2,1,0:T(8,128)(2,1)S(1)} %collective-permute-done.other_ref, bf16[896,256]{1,0:T(8,128)(2,1)S(1)} %get-tuple-element.12.high_ref, ...), custom_call_target="tpu_custom_call" | custom-call | tf_op jit(solution)/shard_map/solve/pallas_call | solution.py:375
  60.9 11.6 %all_to_all.22 = f32[32,7,128]{2,1,0:T(8,128)S(1)} all-to-all(f32[32,7,128]{2,1,0:T(8,128)S(1)} %get-tuple-element.14), channel_id=1, replica_groups=mesh['chip'=16,'core'=2,'basis'=4] {'chip','core'}, dimensions={0} | all-to-all | bytes 229376 | tf_op jit(solution)/shard_map/all_to_all | solution.py:409
  72.5 0.7 reshape.22
  (1 shorter events, 0.0 us)
Async XLA Ops:
  2.5 15.2 %all-to-all-start = ((bf16[16,72,128]{2,1,0:T(8,128)(2,1)}), bf16[16,72,128]{2,1,0:T(8,128)(2,1)S(1)}, u32[]{:S(2)}, u32[]{:S(2)}) async-start(bf16[16,72,128]{2,1,0:T(8,128)(2,1)} %atomic.1), calls=%async_computation | async-start | bytes 589824 | tf_op jit(solution)/shard_map/all_to_all | solution.py:399
  17.7 3.4 %collective-permute-start = (bf16[16,72,128]{2,1,0:T(8,128)(2,1)S(1)}, bf16[16,72,128]{2,1,0:T(8,128)(2,1)S(1)}, u32[]{:S(2)}, u32[]{:S(2)}) collective-permute-start(bf16[16,72,128]{2,1,0:T(8,128)(2,1)S(1)} %all-to-all-done.own_ref), channel_id=1, source_target_pairs={{0,4},{4,0},{1,5},{5,1},{2,6},{6,2},{3,7},{7,3},{8,12},{12,8},{9,1... | collective-permute-start | bytes 884744 | tf_op jit(solution)/shard_map/ppermute | solution.py:389

commit v3 on v2

--- a/solution.py
+++ b/solution.py
@@ -25,7 +25,8 @@
 BLOCK = LOCAL * MAXAT
 PACKED = 72
 CODE, COUNT, ENERGY = 64, 65, 66
-GROUP = 32
+GROUP = 64
+FLAGS = 16
 
 STRUCT = ("chip", "core")
 CUTOFF = 5.0
@@ -59,34 +60,30 @@
             radial.append(envelope)
         else:
             radial.append(envelope * cosine((jnp.float32(math.pi) * jnp.float32(order)) * ratio))
+    lane = lax.broadcasted_iota(jnp.int32, (SPECIES, LANES), 1)
+    row = lax.broadcasted_iota(jnp.int32, (SPECIES, LANES), 0)
+    center = jnp.where(species == row, 1.0, 0.0).astype(jnp.bfloat16)
+    pattern = pattern_ref[...].astype(jnp.float32).astype(jnp.bfloat16)
+    allowed = lax.dot_general(pattern, center, (((0,), (0,)), ((), ())), preferred_element_type=jnp.float32)
     rows = []
     for element in range(SPECIES):
-        allowed = jnp.zeros(species.shape, jnp.float32)
-        for center in range(SPECIES):
-            seen = pattern_ref[center, element].astype(jnp.float32)
-            allowed = jnp.where(species == center, seen, allowed)
-        match = jnp.where(nbr == element, allowed, 0.0)
+        match = jnp.where(nbr == element, allowed[element : element + 1], 0.0)
         for order in range(RADIAL):
             rows.append(jnp.sum(match * radial[order], axis=0, keepdims=True))
     atomic = jnp.concatenate(rows, axis=0).astype(jnp.bfloat16)
 
-    lane = lax.broadcasted_iota(jnp.int32, (1, LANES), 1)
-    slots = lane % MAXAT
-    per_atom = jnp.zeros((1, LANES), jnp.int32)
-    count = jnp.zeros((1, LANES), jnp.float32)
-    energy = jnp.zeros((1, LANES), jnp.float32)
-    for structure in range(LOCAL):
-        amount = counts_ref[structure]
-        per_atom = jnp.where(lane // MAXAT == structure, amount, per_atom)
-        count = jnp.where(lane == structure, amount.astype(jnp.float32), count)
-        energy = jnp.where(lane == structure, energies_ref[structure], energy)
-    code = jnp.where(slots < per_atom, species, SPECIES).astype(jnp.float32)
-    parts = [code, count]
+    small = [counts_ref[...].astype(jnp.float32)]
+    energy = energies_ref[...]
     for _ in range(3):
-        part = energy.astype(jnp.bfloat16).astype(jnp.float32)
-        parts.append(part)
-        energy = energy - part
-    parts.append(jnp.zeros((PACKED - CHANNELS - len(parts), LANES), jnp.float32))
+        small.append(energy.astype(jnp.bfloat16).astype(jnp.float32))
+        energy = energy - small[-1]
+    small = jnp.concatenate(small + [jnp.zeros((4, LOCAL), jnp.float32)], axis=0).astype(jnp.bfloat16)
+    spots = jnp.concatenate([lane // MAXAT == row, lane == row], axis=1)
+    small = jnp.dot(small, jnp.where(spots, 1.0, 0.0).astype(jnp.bfloat16), preferred_element_type=jnp.float32)
+    slots = (lane[:1] % MAXAT).astype(jnp.float32)
+    code = jnp.where(slots < small[:1, :LANES], species, SPECIES).astype(jnp.float32)
+    parts = [code, small[:4, LANES:]]
+    parts.append(jnp.zeros((PACKED - CHANNELS - 5, LANES), jnp.float32))
     packed = jnp.concatenate([atomic, jnp.concatenate(parts, axis=0).astype(jnp.bfloat16)], axis=0)
     for copy in range(out_ref.shape[0]):
         out_ref[copy, :, :] = packed
@@ -94,14 +91,13 @@
 
 def atomic_call(dist, nbr_species, species, counts, pattern, energies, copies):
     vmem = pl.BlockSpec(memory_space=pltpu.VMEM)
-    smem = pl.BlockSpec(memory_space=pltpu.SMEM)
     return pl.pallas_call(
         atomic_kernel,
         out_shape=jax.ShapeDtypeStruct((copies, PACKED, LANES), jnp.bfloat16),
-        in_specs=[vmem, vmem, vmem, smem, smem, smem],
+        in_specs=[vmem] * 6,
         out_specs=vmem,
         name="atomic",
-    )(dist, nbr_species, species.reshape(1, -1), counts, pattern, energies)
+    )(dist, nbr_species, species.reshape(1, -1), counts.reshape(1, -1), pattern, energies.reshape(1, -1))
 
 
 def maps_kernel(maps_ref, out_ref):
@@ -134,39 +130,56 @@
     return core, core * chips + lax.axis_index("chip"), jnp.where(struct < owners, element, SPECIES + 1)
 
 
-def upto_each(element, atoms_ref):
+def share_out(element, atoms_ref):
     codes = atoms_ref[:, CODE, :].astype(jnp.float32)
     lane = lax.broadcasted_iota(jnp.int32, codes.shape, 1)
+    slot, structure = lane % MAXAT, (lane // MAXAT).astype(jnp.float32)
     chosen = jnp.where(codes == element, 1.0, 0.0)
-    upto = chosen
+    upto, since = chosen, chosen
     for reach in (1, 2, 4, 8):
-        upto = upto + jnp.where(lane % MAXAT >= reach, pltpu.roll(upto, reach, 1), 0.0)
-    return chosen, upto
-
-
-def move_atoms(chosen, upto, atoms_ref, ranked_ref):
-    structure = lax.broadcasted_iota(jnp.int32, chosen.shape, 1) // MAXAT
-    target = jnp.where(chosen > 0.0, (upto - 1.0) * LOCAL + structure.astype(jnp.float32), -1.0).astype(jnp.bfloat16)
+        upto = upto + jnp.where(slot >= reach, pltpu.roll(upto, reach, 1), 0.0)
+        since = since + jnp.where(slot < MAXAT - reach, pltpu.roll(since, LANES - reach, 1), 0.0)
+    amount = upto + since - chosen
+    partner = pltpu.roll(amount, codes.shape[0] // 2, 0)
+    held = jnp.floor((amount + partner + 1.0) * 0.5)
+    rank = upto - 1.0
+    stays = jnp.where((chosen > 0.0) & (rank < held), rank * LOCAL + structure, -1.0)
+    leaves = jnp.where((chosen > 0.0) & (rank >= held), (partner + rank - held) * LOCAL + structure, -1.0)
+    return stays.astype(jnp.bfloat16), leaves.astype(jnp.bfloat16), held
+
+
+def move_atoms(stays, leaves, atoms_ref, ranked_ref):
+    chips = atoms_ref.shape[0]
     rows = lax.broadcasted_iota(jnp.int32, (BLOCK, LANES), 0).astype(jnp.float32).astype(jnp.bfloat16)
     one, zero = jnp.ones(rows.shape, jnp.bfloat16), jnp.zeros(rows.shape, jnp.bfloat16)
-    for chip in range(atoms_ref.shape[0]):
-        move = jnp.where(jnp.broadcast_to(target[chip : chip + 1, :], rows.shape) == rows, one, zero)
-        moved = lax.dot_general(
-            move, atoms_ref[chip, :CHANNELS, :], (((1,), (1,)), ((), ())), preferred_element_type=jnp.float32
-        )
+    flags = jnp.concatenate([one[:FLAGS], zero[:FLAGS]], axis=1)
+
+    def hits(target):
+        return jnp.where(jnp.broadcast_to(target, rows.shape) == rows, one, zero)
+
+    for chip in range(0, chips, 2):
+        pair = []
+        for to in (chip, chip + 1):
+            source = (to + chips // 2) % chips
+            move = jnp.concatenate([hits(stays[to : to + 1, :]), hits(leaves[source : source + 1, :])], axis=1)
+            atoms = jnp.concatenate([atoms_ref[to, :CHANNELS, :], atoms_ref[source, :CHANNELS, :]], axis=1)
+            atoms = jnp.concatenate([atoms, flags], axis=0)
+            pair.append(lax.dot_general(move, atoms, (((1,), (1,)), ((), ())), preferred_element_type=jnp.float32))
         for rank in range(MAXAT):
-            ranked_ref[rank, chip * LOCAL : (chip + 1) * LOCAL, :] = moved[rank * LOCAL : (rank + 1) * LOCAL]
+            tile = jnp.concatenate([moved[rank * LOCAL : (rank + 1) * LOCAL] for moved in pair], axis=0)
+            ranked_ref[rank, chip * LOCAL : (chip + 2) * LOCAL, :] = tile.astype(jnp.bfloat16)
 
 
 def ranked_kernel(own_ref, ranked_ref):
-    move_atoms(*upto_each(place()[2].astype(jnp.float32), own_ref), own_ref, ranked_ref)
+    stays, leaves, _ = share_out(place()[2].astype(jnp.float32), own_ref)
+    move_atoms(stays, leaves, own_ref, ranked_ref)
 
 
 def ranked_call(own):
     vmem = pl.BlockSpec(memory_space=pltpu.VMEM)
     return pl.pallas_call(
         ranked_kernel,
-        out_shape=jax.ShapeDtypeStruct((MAXAT, own.shape[0] * LOCAL, CHANNELS), jnp.float32),
+        out_shape=jax.ShapeDtypeStruct((MAXAT, own.shape[0] * LOCAL, CHANNELS + FLAGS), jnp.bfloat16),
         in_specs=[vmem],
         out_specs=vmem,
         compiler_params=pltpu.CompilerParams(vmem_limit_bytes=8 * 1024 * 1024),
@@ -175,14 +188,17 @@
     )(own)
 
 
-def design_kernel(own_ref, other_ref, first_ref, maps_ref, high_ref, low_ref, gram_ref, second_ref, design_ref):
+def design_kernel(own_ref, other_ref, first_ref, maps_ref, high_ref, low_ref, gram_ref, second_ref, design_ref, crossed_ref):
     core, _, element = place()
     element = element.astype(jnp.float32)
-    chosen, upto = upto_each(element, other_ref)
-    ranks = jnp.max(jnp.maximum(upto, upto_each(element, own_ref)[1])).astype(jnp.int32)
-    move_atoms(chosen, upto, other_ref, second_ref)
+    stays, leaves, held = share_out(element, other_ref)
+    ranks = jnp.max(jnp.maximum(held, share_out(element, own_ref)[2])).astype(jnp.int32)
+    move_atoms(stays, leaves, other_ref, second_ref)
     over = (((1,), (1,)), ((), ()))
     design_ref[...] = jnp.zeros(design_ref.shape, jnp.float32)
+    crossed_ref[...] = jnp.zeros(crossed_ref.shape, jnp.float32)
+    pick = lax.broadcasted_iota(jnp.int32, (16, CHANNELS + FLAGS), 1) == CHANNELS
+    pick = jnp.where(pick, 1.0, 0.0).astype(jnp.bfloat16)
 
     def terms(atoms, left):
         columns = maps_ref[left * FACTORS : (left + GROUP) * FACTORS, :]
@@ -197,9 +213,19 @@
         for rank in range(amount):
             own, other = first_ref[first + rank], second_ref[first + rank]
             halves = [jnp.where(core == 0, own, other), jnp.where(core == 0, other, own)]
-            atoms.append(jnp.concatenate(halves, axis=0).astype(jnp.bfloat16))
+            operand = jnp.concatenate(halves, axis=0)
+            flag = lax.dot_general(pick, operand, over, preferred_element_type=jnp.float32)
+            mine = jnp.broadcast_to(flag[:1], (GROUP, STRUCTS)) > 0.5
+            atoms.append((operand[:, :CHANNELS], mine))
         for left in range(0, WIDTH, GROUP):
-            design_ref[left : left + GROUP, :] += sum(terms(operand, left) for operand in atoms)
+            kept = crossed = None
+            for operand, mine in atoms:
+                product = terms(operand, left)
+                here, there = jnp.where(mine, product, 0.0), jnp.where(mine, 0.0, product)
+                kept = here if kept is None else kept + here
+                crossed = there if crossed is None else crossed + there
+            design_ref[left : left + GROUP, :] += kept
+            crossed_ref[left : left + GROUP, :] += crossed
 
     def add_fours(turn, carry):
         add_ranks(turn * 4, 4)
@@ -215,7 +241,8 @@
     def _():
         add_ranks(ranks - 1, 1)
 
-    design = design_ref[...]
+    crossed = [pltpu.roll(crossed_ref[:, at : at + LANES], LANES // 2, 1) for at in range(0, STRUCTS, LANES)]
+    design = design_ref[...] + jnp.concatenate(crossed, axis=1)
     high = design.astype(jnp.bfloat16)
     low = (design - high.astype(jnp.float32)).astype(jnp.bfloat16)
     high_ref[...] = high
@@ -240,7 +267,8 @@
         in_specs=[vmem] * 4,
         out_specs=(vmem, vmem, vmem),
         scratch_shapes=[
-            pltpu.VMEM((MAXAT, STRUCTS // 2, CHANNELS), jnp.float32),
+            pltpu.VMEM((MAXAT, STRUCTS // 2, CHANNELS + FLAGS), jnp.bfloat16),
+            pltpu.VMEM((WIDTH, STRUCTS), jnp.float32),
             pltpu.VMEM((WIDTH, STRUCTS), jnp.float32),
         ],
         compiler_params=pltpu.CompilerParams(vmem_limit_bytes=24 * 1024 * 1024),
@@ -367,7 +395,7 @@
     for copy in range(coefficients_ref.shape[0]):
         coefficients_ref[copy] = rows
     direction = jnp.broadcast_to(left * math.sqrt(STRUCTS), (8, STRUCTS))
-    direction_ref[...] = pltpu.roll(direction, STRUCTS - number * LOCAL, 1)[:1, :LOCAL]
+    direction_ref[...] = pltpu.roll(direction, lax.rem(STRUCTS - number * LOCAL, STRUCTS), 1)[:1, :LOCAL]
 
 
 def solve_call(gram, own, other, high, low, copies):

time: 73.6 us -> 72.5 us (0.985)
  Pallas kernels: 12.2 us -> 10.7 us
    pallas_call x1, Pallas kernels: 7.27 us -> 5.73 us  [design_call(): pl.pallas_call(design_kernel, out_shape=(jax.ShapeDtypeStruct((WIDTH, STR...]
where the time goes in v3:
time: 72.5 us; the launch traced here: 72.1 us
  blocking collectives  42.5 us (59%)
  Pallas kernels  10.7 us (15%)
  starting transfers between devices  9.81 us (14%)
  waiting for transfers between devices  6.66 us (9%)
  local copies, waits for them, and re-layouts  1.72 us (2%)
    all_to_all x1, blocking collectives, body(): lax.all_to_all(gram.reshape(lax.axis_size(everyone), -1, LANES), everyone...  15.8 us
    all_to_all x1, blocking collectives, body(): gram = lax.all_to_all(total_call(parts), everyone, 0, 0).reshape(-1, LANES)  15.2 us
    all_to_all x1, blocking collectives, body(): values = lax.all_to_all(values, STRUCT, 0, 0)  11.6 us
    all_to_all x1, starting transfers between devices, body(): own = lax.all_to_all(packed, 'chip', 0, 0)  7.58 us
    all_to_all x1, waiting for transfers between devices, body(): own = lax.all_to_all(packed, 'chip', 0, 0)  6.17 us
    pallas_call x1, Pallas kernels, design_call(): pl.pallas_call(design_kernel, out_shape=(jax.ShapeDtypeStruct((WIDTH, STR...  5.73 us
    ppermute x1, starting transfers between devices, swap(): return lax.ppermute(value, 'core', [(0, 1), (1, 0)])  2.23 us
    pallas_call x1, Pallas kernels, solve_call(): pl.pallas_call(solve_kernel, out_shape=(jax.ShapeDtypeStruct((copies, WID...  1.98 us
  transfers between devices with their start and end apart: 2, of which 2 were waited for; matrix products, arithmetic and copies ran while one was open for 1% of the time, Pallas kernels for 1%

profile of v3, /device:TPU:1, one launch (start us, length us, event | category | flops | bytes accessed | tf_op | source)
XLA Modules:
  0.0 72.1 jit_solution(17489659333344849258)
XLA Ops:
  0.6 1.8 %atomic.1 = bf16[16,72,128]{2,1,0:T(8,128)(2,1)} custom-call(f32[32,128]{1,0:T(8,128)} %dist_ref.1, s32[32,128]{1,0:T(8,128)} %nbr_ref.1, s32[1,128]{1,0:T(1,128)} %bitcast.8, s32[1,8]{1,0:T(1,128)} %bitcast.9, s32[8,8]{1,0:T(8,128)} %pattern_ref.1, f32[1,8]{1,0:T(1,128)} %bitcast.10), custom_call_target="tpu_custom_call" | custom-call | tf_op jit(solution)/shard_map/atomic/pallas_call | solution.py:94
  2.5 7.6 %all-to-all-start = ((bf16[16,72,128]{2,1,0:T(8,128)(2,1)}), bf16[16,72,128]{2,1,0:T(8,128)(2,1)S(1)}, u32[]{:S(2)}, u32[]{:S(2)}) async-start(bf16[16,72,128]{2,1,0:T(8,128)(2,1)} %atomic.1), calls=%async_computation | async-start | bytes 589824 | tf_op jit(solution)/shard_map/all_to_all | solution.py:427
  10.1 1.1 %constant_dynamic-slice_fusion.maps_ref = bf16[4,64,896]{2,1,0:T(8,128)(2,1)S(1)} fusion(bf16[4,64,25088]{2,1,0:T(8,128)(2,1)} %param.12, s32[]{:T(128)S(6)} %select_n.3), kind=kLoop, calls=%fused_computation | loop fusion | bytes 917508 | tf_op jit(solution)/shard_map/dynamic_slice | solution.py:428
  11.1 0.3 maps.1.maps_ref
  11.4 6.2 %all-to-all-done.own_ref = bf16[16,72,128]{2,1,0:T(8,128)(2,1)S(1)} async-done(((bf16[16,72,128]{2,1,0:T(8,128)(2,1)}), bf16[16,72,128]{2,1,0:T(8,128)(2,1)S(1)}, u32[]{:S(2)}, u32[]{:S(2)}) %all-to-all-start) | async-done | bytes 294944 | tf_op jit(solution)/shard_map/all_to_all | solution.py:427
  17.6 2.2 %collective-permute-start = (bf16[16,72,128]{2,1,0:T(8,128)(2,1)S(1)}, bf16[16,72,128]{2,1,0:T(8,128)(2,1)S(1)}, u32[]{:S(2)}, u32[]{:S(2)}) collective-permute-start(bf16[16,72,128]{2,1,0:T(8,128)(2,1)S(1)} %all-to-all-done.own_ref), channel_id=1, source_target_pairs={{0,4},{4,0},{1,5},{5,1},{2,6},{6,2},{3,7},{7,3},{8,12},{12,8},{9,1... | collective-permute-start | bytes 884744 | tf_op jit(solution)/shard_map/ppermute | solution.py:417
  19.8 0.7 ranked.1.first_ref
  20.6 0.5 collective-permute-done.other_ref
  21.0 5.7 %design.1 = (bf16[896,256]{1,0:T(8,128)(2,1)S(1)}, bf16[896,256]{1,0:T(8,128)(2,1)S(1)}, f32[512,128]{1,0:T(8,128)S(1)}) custom-call(bf16[16,72,128]{2,1,0:T(8,128)(2,1)S(1)} %all-to-all-done.own_ref, bf16[16,72,128]{2,1,0:T(8,128)(2,1)S(1)} %collective-permute-done.other_ref, bf16[16,128,80]{2,1,0:T(8,128)(2,1)S(1)} %ranked.1.first_ref, ...), custom_call_target="tpu_custom_call" | custom-call | tf_op jit(solution)/shard_map/design/pallas_call | solution.py:260
  26.8 15.8 %all_to_all.20.parts_ref = f32[128,4,128]{2,1,0:T(4,128)S(1)} all-to-all(f32[128,4,128]{2,1,0:T(4,128)S(1)} %bitcast.7), channel_id=1, replica_groups=mesh['chip'=16,'core'=2,'basis'=4] {'chip','core','basis'}, dimensions={0} | all-to-all | bytes 524288 | tf_op jit(solution)/shard_map/all_to_all | solution.py:434
  42.6 0.2 total.1
  42.7 15.2 %all_to_all.21 = f32[128,4,128]{2,1,0:T(4,128)S(1)} all-to-all(f32[128,4,128]{2,1,0:T(4,128)S(1)} %total.1), channel_id=1, replica_groups=mesh['chip'=16,'core'=2,'basis'=4] {'chip','core','basis'}, dimensions={0} | all-to-all | bytes 524288 | tf_op jit(solution)/shard_map/all_to_all | solution.py:435
  57.9 2.0 %solve.1 = (f32[32,7,128]{2,1,0:T(8,128)S(1)}, f32[1,8]{1,0:T(1,128)}) custom-call(f32[512,128]{1,0:T(8,128)S(1)} %bitcast.6, bf16[16,72,128]{2,1,0:T(8,128)(2,1)S(1)} %all-to-all-done.own_ref, bf16[16,72,128]{2,1,0:T(8,128)(2,1)S(1)} %collective-permute-done.other_ref, bf16[896,256]{1,0:T(8,128)(2,1)S(1)} %get-tuple-element.12.high_ref, ...), custom_call_target="tpu_custom_call" | custom-call | tf_op jit(solution)/shard_map/solve/pallas_call | solution.py:403
  59.9 11.6 %all_to_all.22 = f32[32,7,128]{2,1,0:T(8,128)S(1)} all-to-all(f32[32,7,128]{2,1,0:T(8,128)S(1)} %get-tuple-element.14), channel_id=1, replica_groups=mesh['chip'=16,'core'=2,'basis'=4] {'chip','core'}, dimensions={0} | all-to-all | bytes 229376 | tf_op jit(solution)/shard_map/all_to_all | solution.py:437
  71.5 0.7 reshape.30
  (1 shorter events, 0.0 us)
Async XLA Ops:
  2.5 15.2 %all-to-all-start = ((bf16[16,72,128]{2,1,0:T(8,128)(2,1)}), bf16[16,72,128]{2,1,0:T(8,128)(2,1)S(1)}, u32[]{:S(2)}, u32[]{:S(2)}) async-start(bf16[16,72,128]{2,1,0:T(8,128)(2,1)} %atomic.1), calls=%async_computation | async-start | bytes 589824 | tf_op jit(solution)/shard_map/all_to_all | solution.py:427
  17.6 3.4 %collective-permute-start = (bf16[16,72,128]{2,1,0:T(8,128)(2,1)S(1)}, bf16[16,72,128]{2,1,0:T(8,128)(2,1)S(1)}, u32[]{:S(2)}, u32[]{:S(2)}) collective-permute-start(bf16[16,72,128]{2,1,0:T(8,128)(2,1)S(1)} %all-to-all-done.own_ref), channel_id=1, source_target_pairs={{0,4},{4,0},{1,5},{5,1},{2,6},{6,2},{3,7},{7,3},{8,12},{12,8},{9,1... | collective-permute-start | bytes 884744 | tf_op jit(solution)/shard_map/ppermute | solution.py:417

commit v4 on v3

--- a/solution.py
+++ b/solution.py
@@ -195,8 +195,6 @@
     ranks = jnp.max(jnp.maximum(held, share_out(element, own_ref)[2])).astype(jnp.int32)
     move_atoms(stays, leaves, other_ref, second_ref)
     over = (((1,), (1,)), ((), ()))
-    design_ref[...] = jnp.zeros(design_ref.shape, jnp.float32)
-    crossed_ref[...] = jnp.zeros(crossed_ref.shape, jnp.float32)
     pick = lax.broadcasted_iota(jnp.int32, (16, CHANNELS + FLAGS), 1) == CHANNELS
     pick = jnp.where(pick, 1.0, 0.0).astype(jnp.bfloat16)
 
@@ -208,7 +206,7 @@
             product = product * values[factor * GROUP : (factor + 1) * GROUP]
         return product
 
-    def add_ranks(first, amount):
+    def add_ranks(first, amount, fresh):
         atoms = []
         for rank in range(amount):
             own, other = first_ref[first + rank], second_ref[first + rank]
@@ -224,23 +222,28 @@
                 here, there = jnp.where(mine, product, 0.0), jnp.where(mine, 0.0, product)
                 kept = here if kept is None else kept + here
                 crossed = there if crossed is None else crossed + there
-            design_ref[left : left + GROUP, :] += kept
-            crossed_ref[left : left + GROUP, :] += crossed
+            rows = slice(left, left + GROUP)
+            design_ref[rows, :] = kept if fresh else design_ref[rows, :] + kept
+            crossed_ref[rows, :] = crossed if fresh else crossed_ref[rows, :] + crossed
+
+    odd = ranks % 4
+
+    @pl.when(odd == 0)
+    def _():
+        design_ref[...] = jnp.zeros(design_ref.shape, jnp.float32)
+        crossed_ref[...] = jnp.zeros(crossed_ref.shape, jnp.float32)
+
+    for amount in range(1, 4):
+
+        @pl.when(odd == amount)
+        def _():
+            add_ranks(0, amount, True)
 
     def add_fours(turn, carry):
-        add_ranks(turn * 4, 4)
+        add_ranks(odd + turn * 4, 4, False)
         return carry
 
     lax.fori_loop(0, ranks // 4, add_fours, 0)
-
-    @pl.when(ranks % 4 >= 2)
-    def _():
-        add_ranks(ranks // 4 * 4, 2)
-
-    @pl.when(ranks % 2 == 1)
-    def _():
-        add_ranks(ranks - 1, 1)
-
     crossed = [pltpu.roll(crossed_ref[:, at : at + LANES], LANES // 2, 1) for at in range(0, STRUCTS, LANES)]
     design = design_ref[...] + jnp.concatenate(crossed, axis=1)
     high = design.astype(jnp.bfloat16)
@@ -430,7 +433,7 @@
     other = swap(own)
     ranked = ranked_call(own)
     high, low, gram = design_call(own, other, ranked, maps)
-    everyone = ("chip", "core", "basis")
+    everyone = ("basis", "chip", "core")
     parts = lax.all_to_all(gram.reshape(lax.axis_size(everyone), -1, LANES), everyone, 0, 0)
     gram = lax.all_to_all(total_call(parts), everyone, 0, 0).reshape(-1, LANES)
     values, direction = solve_call(gram, own, other, high, low, structs)

time: 72.5 us -> 73.1 us (level); the launches traced: 72.1 us -> 73.6 us
  blocking collectives: 42.5 us -> 46.9 us
  Pallas kernels: 10.7 us -> 7.82 us
    all_to_all x1, blocking collectives: 15.8 us -> 20.1 us  [body(): lax.all_to_all(gram.reshape(lax.axis_size(everyone), -1, LANES), everyone...]
    pallas_call x1, Pallas kernels: 5.73 us -> 2.82 us  [design_call(): pl.pallas_call(design_kernel, out_shape=(jax.ShapeDtypeStruct((WIDTH, STR...]
where the time goes in v4:
time: 73.1 us; the launch traced here: 73.6 us
  blocking collectives  46.9 us (64%)
  starting transfers between devices  9.81 us (13%)
  Pallas kernels  7.82 us (11%)
  waiting for transfers between devices  6.66 us (9%)
  local copies, waits for them, and re-layouts  1.72 us (2%)
    all_to_all x1, blocking collectives, body(): lax.all_to_all(gram.reshape(lax.axis_size(everyone), -1, LANES), everyone...  20.1 us
    all_to_all x1, blocking collectives, body(): gram = lax.all_to_all(total_call(parts), everyone, 0, 0).reshape(-1, LANES)  15.2 us
    all_to_all x1, blocking collectives, body(): values = lax.all_to_all(values, STRUCT, 0, 0)  11.6 us
    all_to_all x1, starting transfers between devices, body(): own = lax.all_to_all(packed, 'chip', 0, 0)  7.58 us
    all_to_all x1, waiting for transfers between devices, body(): own = lax.all_to_all(packed, 'chip', 0, 0)  6.17 us
    pallas_call x1, Pallas kernels, design_call(): pl.pallas_call(design_kernel, out_shape=(jax.ShapeDtypeStruct((WIDTH, STR...  2.82 us
    ppermute x1, starting transfers between devices, swap(): return lax.ppermute(value, 'core', [(0, 1), (1, 0)])  2.23 us
    pallas_call x1, Pallas kernels, solve_call(): pl.pallas_call(solve_kernel, out_shape=(jax.ShapeDtypeStruct((copies, WID...  1.98 us
  transfers between devices with their start and end apart: 2, of which 2 were waited for; matrix products, arithmetic and copies ran while one was open for 1% of the time, Pallas kernels for 1%

profile of v4, /device:TPU:1, one launch (start us, length us, event | category | flops | bytes accessed | tf_op | source)
XLA Modules:
  0.0 73.6 jit_solution(13862524824986864964)
XLA Ops:
  0.6 1.8 %atomic.1 = bf16[16,72,128]{2,1,0:T(8,128)(2,1)} custom-call(f32[32,128]{1,0:T(8,128)} %dist_ref.1, s32[32,128]{1,0:T(8,128)} %nbr_ref.1, s32[1,128]{1,0:T(1,128)} %bitcast.8, s32[1,8]{1,0:T(1,128)} %bitcast.9, s32[8,8]{1,0:T(8,128)} %pattern_ref.1, f32[1,8]{1,0:T(1,128)} %bitcast.10), custom_call_target="tpu_custom_call" | custom-call | tf_op jit(solution)/shard_map/atomic/pallas_call | solution.py:94
  2.5 7.6 %all-to-all-start = ((bf16[16,72,128]{2,1,0:T(8,128)(2,1)}), bf16[16,72,128]{2,1,0:T(8,128)(2,1)S(1)}, u32[]{:S(2)}, u32[]{:S(2)}) async-start(bf16[16,72,128]{2,1,0:T(8,128)(2,1)} %atomic.1), calls=%async_computation | async-start | bytes 589824 | tf_op jit(solution)/shard_map/all_to_all | solution.py:430
  10.1 1.1 %constant_dynamic-slice_fusion.maps_ref = bf16[4,64,896]{2,1,0:T(8,128)(2,1)S(1)} fusion(bf16[4,64,25088]{2,1,0:T(8,128)(2,1)} %param.12, s32[]{:T(128)S(6)} %select_n.3), kind=kLoop, calls=%fused_computation | loop fusion | bytes 917508 | tf_op jit(solution)/shard_map/dynamic_slice | solution.py:431
  11.1 0.3 maps.1.maps_ref
  11.4 6.2 %all-to-all-done.own_ref = bf16[16,72,128]{2,1,0:T(8,128)(2,1)S(1)} async-done(((bf16[16,72,128]{2,1,0:T(8,128)(2,1)}), bf16[16,72,128]{2,1,0:T(8,128)(2,1)S(1)}, u32[]{:S(2)}, u32[]{:S(2)}) %all-to-all-start) | async-done | bytes 294944 | tf_op jit(solution)/shard_map/all_to_all | solution.py:430
  17.6 2.2 %collective-permute-start = (bf16[16,72,128]{2,1,0:T(8,128)(2,1)S(1)}, bf16[16,72,128]{2,1,0:T(8,128)(2,1)S(1)}, u32[]{:S(2)}, u32[]{:S(2)}) collective-permute-start(bf16[16,72,128]{2,1,0:T(8,128)(2,1)S(1)} %all-to-all-done.own_ref), channel_id=1, source_target_pairs={{0,4},{4,0},{1,5},{5,1},{2,6},{6,2},{3,7},{7,3},{8,12},{12,8},{9,1... | collective-permute-start | bytes 884744 | tf_op jit(solution)/shard_map/ppermute | solution.py:420
  19.8 0.7 ranked.1.first_ref
  20.6 0.5 collective-permute-done.other_ref
  21.0 2.8 %design.1 = (bf16[896,256]{1,0:T(8,128)(2,1)S(1)}, bf16[896,256]{1,0:T(8,128)(2,1)S(1)}, f32[512,128]{1,0:T(8,128)S(1)}) custom-call(bf16[16,72,128]{2,1,0:T(8,128)(2,1)S(1)} %all-to-all-done.own_ref, bf16[16,72,128]{2,1,0:T(8,128)(2,1)S(1)} %collective-permute-done.other_ref, bf16[16,128,80]{2,1,0:T(8,128)(2,1)S(1)} %ranked.1.first_ref, ...), custom_call_target="tpu_custom_call" | custom-call | tf_op jit(solution)/shard_map/design/pallas_call | solution.py:263
  23.9 20.1 %all_to_all.20.parts_ref = f32[128,4,128]{2,1,0:T(4,128)S(1)} all-to-all(f32[128,4,128]{2,1,0:T(4,128)S(1)} %bitcast.7), channel_id=1, replica_groups=mesh['chip'=16,'core'=2,'basis'=4] {'basis','chip','core'}, dimensions={0} | all-to-all | bytes 524288 | tf_op jit(solution)/shard_map/all_to_all | solution.py:437
  43.9 0.2 total.1
  44.1 15.2 %all_to_all.21 = f32[128,4,128]{2,1,0:T(4,128)S(1)} all-to-all(f32[128,4,128]{2,1,0:T(4,128)S(1)} %total.1), channel_id=1, replica_groups=mesh['chip'=16,'core'=2,'basis'=4] {'basis','chip','core'}, dimensions={0} | all-to-all | bytes 524288 | tf_op jit(solution)/shard_map/all_to_all | solution.py:438
  59.3 2.0 %solve.1 = (f32[32,7,128]{2,1,0:T(8,128)S(1)}, f32[1,8]{1,0:T(1,128)}) custom-call(f32[512,128]{1,0:T(8,128)S(1)} %bitcast.6, bf16[16,72,128]{2,1,0:T(8,128)(2,1)S(1)} %all-to-all-done.own_ref, bf16[16,72,128]{2,1,0:T(8,128)(2,1)S(1)} %collective-permute-done.other_ref, bf16[896,256]{1,0:T(8,128)(2,1)S(1)} %get-tuple-element.12.high_ref, ...), custom_call_target="tpu_custom_call" | custom-call | tf_op jit(solution)/shard_map/solve/pallas_call | solution.py:406
  61.3 11.6 %all_to_all.22 = f32[32,7,128]{2,1,0:T(8,128)S(1)} all-to-all(f32[32,7,128]{2,1,0:T(8,128)S(1)} %get-tuple-element.14), channel_id=1, replica_groups=mesh['chip'=16,'core'=2,'basis'=4] {'chip','core'}, dimensions={0} | all-to-all | bytes 229376 | tf_op jit(solution)/shard_map/all_to_all | solution.py:440
  73.0 0.7 reshape.30
  (1 shorter events, 0.0 us)
Async XLA Ops:
  2.5 15.2 %all-to-all-start = ((bf16[16,72,128]{2,1,0:T(8,128)(2,1)}), bf16[16,72,128]{2,1,0:T(8,128)(2,1)S(1)}, u32[]{:S(2)}, u32[]{:S(2)}) async-start(bf16[16,72,128]{2,1,0:T(8,128)(2,1)} %atomic.1), calls=%async_computation | async-start | bytes 589824 | tf_op jit(solution)/shard_map/all_to_all | solution.py:430
  17.6 3.4 %collective-permute-start = (bf16[16,72,128]{2,1,0:T(8,128)(2,1)S(1)}, bf16[16,72,128]{2,1,0:T(8,128)(2,1)S(1)}, u32[]{:S(2)}, u32[]{:S(2)}) collective-permute-start(bf16[16,72,128]{2,1,0:T(8,128)(2,1)S(1)} %all-to-all-done.own_ref), channel_id=1, source_target_pairs={{0,4},{4,0},{1,5},{5,1},{2,6},{6,2},{3,7},{7,3},{8,12},{12,8},{9,1... | collective-permute-start | bytes 884744 | tf_op jit(solution)/shard_map/ppermute | solution.py:420

commit v5 on v4

--- a/solution.py
+++ b/solution.py
@@ -170,8 +170,8 @@
             ranked_ref[rank, chip * LOCAL : (chip + 2) * LOCAL, :] = tile.astype(jnp.bfloat16)
 
 
-def ranked_kernel(own_ref, ranked_ref):
-    stays, leaves, _ = share_out(place()[2].astype(jnp.float32), own_ref)
+def ranked_kernel(own_ref, ranked_ref, held_ref):
+    stays, leaves, held_ref[...] = share_out(place()[2].astype(jnp.float32), own_ref)
     move_atoms(stays, leaves, own_ref, ranked_ref)
 
 
@@ -179,20 +179,23 @@
     vmem = pl.BlockSpec(memory_space=pltpu.VMEM)
     return pl.pallas_call(
         ranked_kernel,
-        out_shape=jax.ShapeDtypeStruct((MAXAT, own.shape[0] * LOCAL, CHANNELS + FLAGS), jnp.bfloat16),
+        out_shape=(
+            jax.ShapeDtypeStruct((MAXAT, own.shape[0] * LOCAL, CHANNELS + FLAGS), jnp.bfloat16),
+            jax.ShapeDtypeStruct((own.shape[0], LANES), jnp.float32),
+        ),
         in_specs=[vmem],
-        out_specs=vmem,
+        out_specs=(vmem, vmem),
         compiler_params=pltpu.CompilerParams(vmem_limit_bytes=8 * 1024 * 1024),
         cost_estimate=pl.CostEstimate(flops=40000000, bytes_accessed=1400000, transcendentals=0),
         name="ranked",
     )(own)
 
 
-def design_kernel(own_ref, other_ref, first_ref, maps_ref, high_ref, low_ref, gram_ref, second_ref, design_ref, crossed_ref):
+def design_kernel(held_ref, other_ref, first_ref, maps_ref, high_ref, low_ref, gram_ref, second_ref, design_ref, crossed_ref):
     core, _, element = place()
     element = element.astype(jnp.float32)
     stays, leaves, held = share_out(element, other_ref)
-    ranks = jnp.max(jnp.maximum(held, share_out(element, own_ref)[2])).astype(jnp.int32)
+    ranks = jnp.max(jnp.maximum(held, held_ref[...])).astype(jnp.int32)
     move_atoms(stays, leaves, other_ref, second_ref)
     over = (((1,), (1,)), ((), ()))
     pick = lax.broadcasted_iota(jnp.int32, (16, CHANNELS + FLAGS), 1) == CHANNELS
@@ -258,7 +261,7 @@
         gram_ref[left // LANES * STRUCTS : (left // LANES + 1) * STRUCTS, :] = gram[:, left : left + LANES]
 
 
-def design_call(own, other, ranked, maps):
+def design_call(held, other, ranked, maps):
     vmem = pl.BlockSpec(memory_space=pltpu.VMEM)
     return pl.pallas_call(
         design_kernel,
@@ -276,7 +279,7 @@
         ],
         compiler_params=pltpu.CompilerParams(vmem_limit_bytes=24 * 1024 * 1024),
         name="design",
-    )(own, other, ranked, maps)
+    )(held, other, ranked, maps)
 
 
 def total_kernel(parts_ref, out_ref):
@@ -431,9 +434,9 @@
     maps = maps_call(lax.dynamic_slice_in_dim(projections, mine * WIDTH, WIDTH, 2))
     own, maps = lax.optimization_barrier((own, maps))
     other = swap(own)
-    ranked = ranked_call(own)
-    high, low, gram = design_call(own, other, ranked, maps)
-    everyone = ("basis", "chip", "core")
+    ranked, held = ranked_call(own)
+    high, low, gram = design_call(held, other, ranked, maps)
+    everyone = ("chip", "core", "basis")
     parts = lax.all_to_all(gram.reshape(lax.axis_size(everyone), -1, LANES), everyone, 0, 0)
     gram = lax.all_to_all(total_call(parts), everyone, 0, 0).reshape(-1, LANES)
     values, direction = solve_call(gram, own, other, high, low, structs)

time: 73.1 us -> 74.8 us (1.023); the launches traced: 73.6 us -> 74.5 us
  Pallas kernels: 7.82 us -> 8.92 us
    pallas_call x1, Pallas kernels: 2.82 us -> 3.92 us  [design_call(): pl.pallas_call(design_kernel, out_shape=(jax.ShapeDtypeStruct((WIDTH, STR...]
where the time goes in v5:
time: 74.8 us; the launch traced here: 74.5 us
  blocking collectives  46.7 us (62%)
  starting transfers between devices  9.81 us (13%)
  Pallas kernels  8.92 us (12%)
  waiting for transfers between devices  6.66 us (9%)
  local copies, waits for them, and re-layouts  1.72 us (2%)
    all_to_all x1, blocking collectives, body(): lax.all_to_all(gram.reshape(lax.axis_size(everyone), -1, LANES), everyone...  20 us
    all_to_all x1, blocking collectives, body(): gram = lax.all_to_all(total_call(parts), everyone, 0, 0).reshape(-1, LANES)  15.2 us
    all_to_all x1, blocking collectives, body(): values = lax.all_to_all(values, STRUCT, 0, 0)  11.6 us
    all_to_all x1, starting transfers between devices, body(): own = lax.all_to_all(packed, 'chip', 0, 0)  7.58 us
    all_to_all x1, waiting for transfers between devices, body(): own = lax.all_to_all(packed, 'chip', 0, 0)  6.17 us
    pallas_call x1, Pallas kernels, design_call(): pl.pallas_call(design_kernel, out_shape=(jax.ShapeDtypeStruct((WIDTH, STR...  3.92 us
    ppermute x1, starting transfers between devices, swap(): return lax.ppermute(value, 'core', [(0, 1), (1, 0)])  2.23 us
    pallas_call x1, Pallas kernels, solve_call(): pl.pallas_call(solve_kernel, out_shape=(jax.ShapeDtypeStruct((copies, WID...  1.98 us
  transfers between devices with their start and end apart: 2, of which 2 were waited for; matrix products, arithmetic and copies ran while one was open for 1% of the time, Pallas kernels for 1%

profile of v5, /device:TPU:1, one launch (start us, length us, event | category | flops | bytes accessed | tf_op | source)
XLA Modules:
  0.0 74.5 jit_solution(11494778656742251857)
XLA Ops:
  0.6 1.8 %atomic.1 = bf16[16,72,128]{2,1,0:T(8,128)(2,1)} custom-call(f32[32,128]{1,0:T(8,128)} %dist_ref.1, s32[32,128]{1,0:T(8,128)} %nbr_ref.1, s32[1,128]{1,0:T(1,128)} %bitcast.8, s32[1,8]{1,0:T(1,128)} %bitcast.9, s32[8,8]{1,0:T(8,128)} %pattern_ref.1, f32[1,8]{1,0:T(1,128)} %bitcast.10), custom_call_target="tpu_custom_call" | custom-call | tf_op jit(solution)/shard_map/atomic/pallas_call | solution.py:94
  2.5 7.6 %all-to-all-start = ((bf16[16,72,128]{2,1,0:T(8,128)(2,1)}), bf16[16,72,128]{2,1,0:T(8,128)(2,1)S(1)}, u32[]{:S(2)}, u32[]{:S(2)}) async-start(bf16[16,72,128]{2,1,0:T(8,128)(2,1)} %atomic.1), calls=%async_computation | async-start | bytes 589824 | tf_op jit(solution)/shard_map/all_to_all | solution.py:433
  10.1 1.1 %constant_dynamic-slice_fusion.maps_ref = bf16[4,64,896]{2,1,0:T(8,128)(2,1)S(1)} fusion(bf16[4,64,25088]{2,1,0:T(8,128)(2,1)} %param.12, s32[]{:T(128)S(6)} %select_n.3), kind=kLoop, calls=%fused_computation | loop fusion | bytes 917508 | tf_op jit(solution)/shard_map/dynamic_slice | solution.py:434
  11.1 0.3 maps.1.maps_ref
  11.4 6.2 %all-to-all-done.own_ref = bf16[16,72,128]{2,1,0:T(8,128)(2,1)S(1)} async-done(((bf16[16,72,128]{2,1,0:T(8,128)(2,1)}), bf16[16,72,128]{2,1,0:T(8,128)(2,1)S(1)}, u32[]{:S(2)}, u32[]{:S(2)}) %all-to-all-start) | async-done | bytes 294944 | tf_op jit(solution)/shard_map/all_to_all | solution.py:433
  17.6 2.2 %collective-permute-start = (bf16[16,72,128]{2,1,0:T(8,128)(2,1)S(1)}, bf16[16,72,128]{2,1,0:T(8,128)(2,1)S(1)}, u32[]{:S(2)}, u32[]{:S(2)}) collective-permute-start(bf16[16,72,128]{2,1,0:T(8,128)(2,1)S(1)} %all-to-all-done.own_ref), channel_id=1, source_target_pairs={{0,4},{4,0},{1,5},{5,1},{2,6},{6,2},{3,7},{7,3},{8,12},{12,8},{9,1... | collective-permute-start | bytes 884744 | tf_op jit(solution)/shard_map/ppermute | solution.py:423
  19.8 0.7 ranked.1
  20.5 0.5 collective-permute-done.other_ref
  21.0 3.9 %design.1 = (bf16[896,256]{1,0:T(8,128)(2,1)S(1)}, bf16[896,256]{1,0:T(8,128)(2,1)S(1)}, f32[512,128]{1,0:T(8,128)S(1)}) custom-call(f32[16,128]{1,0:T(8,128)S(1)} %get-tuple-element.12.held_ref, bf16[16,72,128]{2,1,0:T(8,128)(2,1)S(1)} %collective-permute-done.other_ref, bf16[16,128,80]{2,1,0:T(8,128)(2,1)S(1)} %get-tuple-element.13.first_ref, ...), custom_call_target="tpu_custom_call" | custom-call | tf_op jit(solution)/shard_map/design/pallas_call | solution.py:266
  25.0 20.0 %all_to_all.20.parts_ref = f32[128,4,128]{2,1,0:T(4,128)S(1)} all-to-all(f32[128,4,128]{2,1,0:T(4,128)S(1)} %bitcast.7), channel_id=1, replica_groups=mesh['chip'=16,'core'=2,'basis'=4] {'chip','core','basis'}, dimensions={0} | all-to-all | bytes 524288 | tf_op jit(solution)/shard_map/all_to_all | solution.py:440
  44.9 0.2 total.1
  45.1 15.2 %all_to_all.21 = f32[128,4,128]{2,1,0:T(4,128)S(1)} all-to-all(f32[128,4,128]{2,1,0:T(4,128)S(1)} %total.1), channel_id=1, replica_groups=mesh['chip'=16,'core'=2,'basis'=4] {'chip','core','basis'}, dimensions={0} | all-to-all | bytes 524288 | tf_op jit(solution)/shard_map/all_to_all | solution.py:441
  60.3 2.0 %solve.1 = (f32[32,7,128]{2,1,0:T(8,128)S(1)}, f32[1,8]{1,0:T(1,128)}) custom-call(f32[512,128]{1,0:T(8,128)S(1)} %bitcast.6, bf16[16,72,128]{2,1,0:T(8,128)(2,1)S(1)} %all-to-all-done.own_ref, bf16[16,72,128]{2,1,0:T(8,128)(2,1)S(1)} %collective-permute-done.other_ref, bf16[896,256]{1,0:T(8,128)(2,1)S(1)} %get-tuple-element.16.high_ref, ...), custom_call_target="tpu_custom_call" | custom-call | tf_op jit(solution)/shard_map/solve/pallas_call | solution.py:409
  62.2 11.6 %all_to_all.22 = f32[32,7,128]{2,1,0:T(8,128)S(1)} all-to-all(f32[32,7,128]{2,1,0:T(8,128)S(1)} %get-tuple-element.18), channel_id=1, replica_groups=mesh['chip'=16,'core'=2,'basis'=4] {'chip','core'}, dimensions={0} | all-to-all | bytes 229376 | tf_op jit(solution)/shard_map/all_to_all | solution.py:443
  73.8 0.7 reshape.30
  (1 shorter events, 0.0 us)
Async XLA Ops:
  2.5 15.2 %all-to-all-start = ((bf16[16,72,128]{2,1,0:T(8,128)(2,1)}), bf16[16,72,128]{2,1,0:T(8,128)(2,1)S(1)}, u32[]{:S(2)}, u32[]{:S(2)}) async-start(bf16[16,72,128]{2,1,0:T(8,128)(2,1)} %atomic.1), calls=%async_computation | async-start | bytes 589824 | tf_op jit(solution)/shard_map/all_to_all | solution.py:433
  17.6 3.4 %collective-permute-start = (bf16[16,72,128]{2,1,0:T(8,128)(2,1)S(1)}, bf16[16,72,128]{2,1,0:T(8,128)(2,1)S(1)}, u32[]{:S(2)}, u32[]{:S(2)}) collective-permute-start(bf16[16,72,128]{2,1,0:T(8,128)(2,1)S(1)} %all-to-all-done.own_ref), channel_id=1, source_target_pairs={{0,4},{4,0},{1,5},{5,1},{2,6},{6,2},{3,7},{7,3},{8,12},{12,8},{9,1... | collective-permute-start | bytes 884744 | tf_op jit(solution)/shard_map/ppermute | solution.py:423

commit v6 on v4

--- a/solution.py
+++ b/solution.py
@@ -25,7 +25,7 @@
 BLOCK = LOCAL * MAXAT
 PACKED = 72
 CODE, COUNT, ENERGY = 64, 65, 66
-GROUP = 64
+GROUP = 128
 FLAGS = 16
 
 STRUCT = ("chip", "core")
@@ -433,7 +433,7 @@
     other = swap(own)
     ranked = ranked_call(own)
     high, low, gram = design_call(own, other, ranked, maps)
-    everyone = ("basis", "chip", "core")
+    everyone = ("chip", "core", "basis")
     parts = lax.all_to_all(gram.reshape(lax.axis_size(everyone), -1, LANES), everyone, 0, 0)
     gram = lax.all_to_all(total_call(parts), everyone, 0, 0).reshape(-1, LANES)
     values, direction = solve_call(gram, own, other, high, low, structs)

time: 73.1 us -> 74.1 us (1.014); the launches traced: 73.6 us -> 73 us
  blocking collectives: 46.9 us -> 45.2 us
  Pallas kernels: 7.82 us -> 8.94 us
    all_to_all x1, blocking collectives: 20.1 us -> 18.5 us  [body(): lax.all_to_all(gram.reshape(lax.axis_size(everyone), -1, LANES), everyone...]
    pallas_call x1, Pallas kernels: 2.82 us -> 3.94 us  [design_call(): pl.pallas_call(design_kernel, out_shape=(jax.ShapeDtypeStruct((WIDTH, STR...]
where the time goes in v6:
time: 74.1 us; the launch traced here: 73 us
  blocking collectives  45.2 us (61%)
  starting transfers between devices  9.81 us (13%)
  Pallas kernels  8.94 us (12%)
  waiting for transfers between devices  6.66 us (9%)
  local copies, waits for them, and re-layouts  1.72 us (2%)
    all_to_all x1, blocking collectives, body(): lax.all_to_all(gram.reshape(lax.axis_size(everyone), -1, LANES), everyone...  18.5 us
    all_to_all x1, blocking collectives, body(): gram = lax.all_to_all(total_call(parts), everyone, 0, 0).reshape(-1, LANES)  15.2 us
    all_to_all x1, blocking collectives, body(): values = lax.all_to_all(values, STRUCT, 0, 0)  11.6 us
    all_to_all x1, starting transfers between devices, body(): own = lax.all_to_all(packed, 'chip', 0, 0)  7.58 us
    all_to_all x1, waiting for transfers between devices, body(): own = lax.all_to_all(packed, 'chip', 0, 0)  6.17 us
    pallas_call x1, Pallas kernels, design_call(): pl.pallas_call(design_kernel, out_shape=(jax.ShapeDtypeStruct((WIDTH, STR...  3.94 us
    ppermute x1, starting transfers between devices, swap(): return lax.ppermute(value, 'core', [(0, 1), (1, 0)])  2.23 us
    pallas_call x1, Pallas kernels, solve_call(): pl.pallas_call(solve_kernel, out_shape=(jax.ShapeDtypeStruct((copies, WID...  1.98 us
  transfers between devices with their start and end apart: 2, of which 2 were waited for; matrix products, arithmetic and copies ran while one was open for 1% of the time, Pallas kernels for 1%

profile of v6, /device:TPU:1, one launch (start us, length us, event | category | flops | bytes accessed | tf_op | source)
XLA Modules:
  0.0 73.0 jit_solution(6975555260698893444)
XLA Ops:
  0.6 1.8 %atomic.1 = bf16[16,72,128]{2,1,0:T(8,128)(2,1)} custom-call(f32[32,128]{1,0:T(8,128)} %dist_ref.1, s32[32,128]{1,0:T(8,128)} %nbr_ref.1, s32[1,128]{1,0:T(1,128)} %bitcast.8, s32[1,8]{1,0:T(1,128)} %bitcast.9, s32[8,8]{1,0:T(8,128)} %pattern_ref.1, f32[1,8]{1,0:T(1,128)} %bitcast.10), custom_call_target="tpu_custom_call" | custom-call | tf_op jit(solution)/shard_map/atomic/pallas_call | solution.py:94
  2.5 7.6 %all-to-all-start = ((bf16[16,72,128]{2,1,0:T(8,128)(2,1)}), bf16[16,72,128]{2,1,0:T(8,128)(2,1)S(1)}, u32[]{:S(2)}, u32[]{:S(2)}) async-start(bf16[16,72,128]{2,1,0:T(8,128)(2,1)} %atomic.1), calls=%async_computation | async-start | bytes 589824 | tf_op jit(solution)/shard_map/all_to_all | solution.py:430
  10.1 1.1 %constant_dynamic-slice_fusion.maps_ref = bf16[4,64,896]{2,1,0:T(8,128)(2,1)S(1)} fusion(bf16[4,64,25088]{2,1,0:T(8,128)(2,1)} %param.12, s32[]{:T(128)S(6)} %select_n.3), kind=kLoop, calls=%fused_computation | loop fusion | bytes 917508 | tf_op jit(solution)/shard_map/dynamic_slice | solution.py:431
  11.1 0.3 maps.1.maps_ref
  11.4 6.2 %all-to-all-done.own_ref = bf16[16,72,128]{2,1,0:T(8,128)(2,1)S(1)} async-done(((bf16[16,72,128]{2,1,0:T(8,128)(2,1)}), bf16[16,72,128]{2,1,0:T(8,128)(2,1)S(1)}, u32[]{:S(2)}, u32[]{:S(2)}) %all-to-all-start) | async-done | bytes 294944 | tf_op jit(solution)/shard_map/all_to_all | solution.py:430
  17.6 2.2 %collective-permute-start = (bf16[16,72,128]{2,1,0:T(8,128)(2,1)S(1)}, bf16[16,72,128]{2,1,0:T(8,128)(2,1)S(1)}, u32[]{:S(2)}, u32[]{:S(2)}) collective-permute-start(bf16[16,72,128]{2,1,0:T(8,128)(2,1)S(1)} %all-to-all-done.own_ref), channel_id=1, source_target_pairs={{0,4},{4,0},{1,5},{5,1},{2,6},{6,2},{3,7},{7,3},{8,12},{12,8},{9,1... | collective-permute-start | bytes 884744 | tf_op jit(solution)/shard_map/ppermute | solution.py:420
  19.8 0.7 ranked.1.first_ref
  20.6 0.5 collective-permute-done.other_ref
  21.0 3.9 %design.1 = (bf16[896,256]{1,0:T(8,128)(2,1)S(1)}, bf16[896,256]{1,0:T(8,128)(2,1)S(1)}, f32[512,128]{1,0:T(8,128)S(1)}) custom-call(bf16[16,72,128]{2,1,0:T(8,128)(2,1)S(1)} %all-to-all-done.own_ref, bf16[16,72,128]{2,1,0:T(8,128)(2,1)S(1)} %collective-permute-done.other_ref, bf16[16,128,80]{2,1,0:T(8,128)(2,1)S(1)} %ranked.1.first_ref, ...), custom_call_target="tpu_custom_call" | custom-call | tf_op jit(solution)/shard_map/design/pallas_call | solution.py:263
  25.0 18.5 %all_to_all.20.parts_ref = f32[128,4,128]{2,1,0:T(4,128)S(1)} all-to-all(f32[128,4,128]{2,1,0:T(4,128)S(1)} %bitcast.7), channel_id=1, replica_groups=mesh['chip'=16,'core'=2,'basis'=4] {'chip','core','basis'}, dimensions={0} | all-to-all | bytes 524288 | tf_op jit(solution)/shard_map/all_to_all | solution.py:437
  43.5 0.2 total.1
  43.7 15.2 %all_to_all.21 = f32[128,4,128]{2,1,0:T(4,128)S(1)} all-to-all(f32[128,4,128]{2,1,0:T(4,128)S(1)} %total.1), channel_id=1, replica_groups=mesh['chip'=16,'core'=2,'basis'=4] {'chip','core','basis'}, dimensions={0} | all-to-all | bytes 524288 | tf_op jit(solution)/shard_map/all_to_all | solution.py:438
  58.8 2.0 %solve.1 = (f32[32,7,128]{2,1,0:T(8,128)S(1)}, f32[1,8]{1,0:T(1,128)}) custom-call(f32[512,128]{1,0:T(8,128)S(1)} %bitcast.6, bf16[16,72,128]{2,1,0:T(8,128)(2,1)S(1)} %all-to-all-done.own_ref, bf16[16,72,128]{2,1,0:T(8,128)(2,1)S(1)} %collective-permute-done.other_ref, bf16[896,256]{1,0:T(8,128)(2,1)S(1)} %get-tuple-element.12.high_ref, ...), custom_call_target="tpu_custom_call" | custom-call | tf_op jit(solution)/shard_map/solve/pallas_call | solution.py:406
  60.8 11.6 %all_to_all.22 = f32[32,7,128]{2,1,0:T(8,128)S(1)} all-to-all(f32[32,7,128]{2,1,0:T(8,128)S(1)} %get-tuple-element.14), channel_id=1, replica_groups=mesh['chip'=16,'core'=2,'basis'=4] {'chip','core'}, dimensions={0} | all-to-all | bytes 229376 | tf_op jit(solution)/shard_map/all_to_all | solution.py:440
  72.4 0.7 reshape.30
  (1 shorter events, 0.0 us)
Async XLA Ops:
  2.5 15.2 %all-to-all-start = ((bf16[16,72,128]{2,1,0:T(8,128)(2,1)}), bf16[16,72,128]{2,1,0:T(8,128)(2,1)S(1)}, u32[]{:S(2)}, u32[]{:S(2)}) async-start(bf16[16,72,128]{2,1,0:T(8,128)(2,1)} %atomic.1), calls=%async_computation | async-start | bytes 589824 | tf_op jit(solution)/shard_map/all_to_all | solution.py:430
  17.6 3.4 %collective-permute-start = (bf16[16,72,128]{2,1,0:T(8,128)(2,1)S(1)}, bf16[16,72,128]{2,1,0:T(8,128)(2,1)S(1)}, u32[]{:S(2)}, u32[]{:S(2)}) collective-permute-start(bf16[16,72,128]{2,1,0:T(8,128)(2,1)S(1)} %all-to-all-done.own_ref), channel_id=1, source_target_pairs={{0,4},{4,0},{1,5},{5,1},{2,6},{6,2},{3,7},{7,3},{8,12},{12,8},{9,1... | collective-permute-start | bytes 884744 | tf_op jit(solution)/shard_map/ppermute | solution.py:420
